TPU v7x, 256 devices: a whole 4x4x8 slice. The times are simulated.
256 devices in a mesh: enc: 16 (over y, x), dom: 16 (over z, core).
Axes of the slice: x: 4, y: 4, z: 8, core: 2. Of those that a mesh axis runs over, the one named last changes fastest.
Arguments:
- residual: bfloat16 [4096, 4, 8192], P('enc', None, 'dom'), may hold values from -6 to 6
- weights: int32 [16, 4096], P(None, 'enc'), may hold values from -1 to 1, as said below
- source_pos: int32 [4096], replicated, may hold values from 0 to 4194303, as said below
- receiver_pos: int32 [8192], P('dom'), may hold values from 0 to 4194303, as said below
- wavelet: float32 [4], replicated, may hold values from -4 to 4
- courant: float32 [256, 128, 128], P('dom'), may hold values from 0.05 to 0.2
- fwd_prev: float32 [16, 256, 128, 128], P('enc', 'dom'), may hold values from -6 to 6
- fwd_now: float32 [16, 256, 128, 128], P('enc', 'dom'), may hold values from -6 to 6
- adj_next: float32 [16, 256, 128, 128], P('enc', 'dom'), may hold values from -6 to 6
- adj_now: float32 [16, 256, 128, 128], P('enc', 'dom'), may hold values from -6 to 6
Outputs:
- gradient: float32 [256, 128, 128], P('dom', 'enc')
- fwd_last: float32 [16, 256, 128, 128], P('enc', 'dom')
- adj_first: float32 [16, 256, 128, 128], P('enc', 'dom')
Inputs may be any that keep to these rules, and one draw needn't show every extreme that they name: `weights`: every entry is -1 or 1. `source_pos`: flat cell index over the whole grid. `receiver_pos`: receiver r lies in depth slab r // 512: its flat index lies in [(r // 512) * 16 * 128 * 128, (r // 512 + 1) * 16 * 128 * 128).
All inputs are finite; a program needn't handle non-finite values.
Results may differ from a plain program's by a relative error of at most 0.0003.
Values may be sent and summed in bfloat16 or wider, within the bound.
A program may use at most 128 MiB of HBM per device.

v0:
```python
import functools

import jax
import jax.numpy as jnp
from jax import lax
from jax.experimental import pallas as pl
from jax.experimental.pallas import tpu as pltpu
from jax.sharding import PartitionSpec as P

MESH = pl.DeviceIdType.MESH
F32 = jnp.float32
BF16 = jnp.bfloat16
UNIT = 5040.0
CENTER = 3.0 * -14350.0
RINGS = (8064.0, -1008.0, 128.0, -9.0)
PAD = 8
HALO = 4


def kernel(
    n,
    nd,
    residual,
    weights,
    source_pos,
    receiver_pos,
    wavelet,
    courant,
    fwd_prev,
    fwd_now,
    adj_next,
    adj_now,
    gradient,
    fwd_last,
    adj_first,
    res_v,
    cour_v,
    u_a,
    u_b,
    w_a,
    w_b,
    a_4,
    a_5,
    a_1,
    image_0,
    image_1,
    grad,
    pattern,
    inject,
    band,
    rows_hot,
    cols_hot,
    part,
    parts,
    gsend,
    grecv,
    gout,
    load_sem,
    store_sem,
    enc_send,
    enc_recv,
    halo_send,
    halo_recv,
    grad_send,
    grad_recv,
):
    depth, width, length = cour_v.shape
    shots = weights.shape[1]
    steps = res_v.shape[1]
    recvs = receiver_pos.shape[1]
    shift = width.bit_length() - 1
    e = lax.axis_index("enc")
    d = lax.axis_index("dom")
    inner = pl.ds(HALO, depth)
    body_rows = pl.ds(PAD, width)

    loads = [
        pltpu.make_async_copy(fwd_now.at[0], u_a.at[inner, body_rows, :], load_sem.at[0]),
        pltpu.make_async_copy(adj_now.at[0], a_4, load_sem.at[1]),
        pltpu.make_async_copy(courant, cour_v, load_sem.at[2]),
        pltpu.make_async_copy(residual, res_v, load_sem.at[3]),
        pltpu.make_async_copy(fwd_prev.at[0], u_b.at[inner, body_rows, :], load_sem.at[4]),
        pltpu.make_async_copy(adj_next.at[0], a_5, load_sem.at[5]),
    ]
    for copy in loads:
        copy.start()

    for field in (u_a, u_b, w_a, w_b):
        edge = jnp.zeros((depth + 2 * HALO, PAD, length), F32)
        field[:, pl.ds(0, PAD), :] = edge
        field[:, pl.ds(PAD + width, PAD), :] = edge

        @pl.when(d == 0)
        def _():
            field[pl.ds(0, HALO)] = jnp.zeros((HALO, width + 2 * PAD, length), F32)

        @pl.when(d == nd - 1)
        def _():
            field[pl.ds(HALO + depth, HALO)] = jnp.zeros((HALO, width + 2 * PAD, length), F32)

    barrier = pltpu.get_barrier_semaphore()

    def greet(k, carry):
        pl.semaphore_signal(
            barrier, inc=1, device_id={"enc": lax.rem(e + k, n)}, device_id_type=MESH
        )
        return carry

    lax.fori_loop(1, n, greet, 0)

    @pl.when(d > 0)
    def _():
        pl.semaphore_signal(barrier, inc=1, device_id={"dom": d - 1}, device_id_type=MESH)

    @pl.when(d < nd - 1)
    def _():
        pl.semaphore_signal(barrier, inc=1, device_id={"dom": d + 1}, device_id_type=MESH)

    pl.semaphore_wait(
        barrier, n - 1 + (d > 0).astype(jnp.int32) + (d < nd - 1).astype(jnp.int32)
    )

    def halo_copy(h, source, field, down):
        near = 0 if down else depth - HALO
        if source is field:
            src = field.at[pl.ds(HALO + near, HALO), body_rows, :]
        else:
            src = source.at[0, pl.ds(near, HALO)]
        far = HALO + depth if down else 0
        way = 0 if down else 1
        return pltpu.make_async_remote_copy(
            src_ref=src,
            dst_ref=field.at[pl.ds(far, HALO), body_rows, :],
            send_sem=halo_send.at[h, way],
            recv_sem=halo_recv.at[h, way],
            device_id={"dom": d - 1 if down else d + 1},
            device_id_type=MESH,
        )

    def halo_start(h, source, field):
        @pl.when(d > 0)
        def _():
            halo_copy(h, source, field, True).start()

        @pl.when(d < nd - 1)
        def _():
            halo_copy(h, source, field, False).start()

    def halo_sent(h, source, field):
        @pl.when(d > 0)
        def _():
            halo_copy(h, source, field, True).wait_send()

        @pl.when(d < nd - 1)
        def _():
            halo_copy(h, source, field, False).wait_send()

    def halo_wait(h, source, field):
        @pl.when(d < nd - 1)
        def _():
            halo_copy(h, source, field, True).wait_recv()

        @pl.when(d > 0)
        def _():
            halo_copy(h, source, field, False).wait_recv()

    halo_start(0, fwd_now, u_a)

    loads[1].wait()
    loads[2].wait()

    def scale_tile(j, carry):
        rows = pl.ds(pl.multiple_of(j * 8, 8), 8)
        scaled = cour_v[:, rows, :] * (1.0 / UNIT)
        cour_v[:, rows, :] = scaled
        w_a[inner, pl.ds(pl.multiple_of(j * 8 + PAD, 8), 8), :] = scaled * a_4[:, rows, :]
        return carry

    lax.fori_loop(0, width // 8, scale_tile, 0)
    halo_start(1, w_a, w_a)

    signs = weights[...].astype(F32)
    shot_of = lax.shift_right_logical(lax.broadcasted_iota(jnp.int32, (shots, shots * steps), 1), 2)
    spread = jnp.where(
        shot_of == lax.broadcasted_iota(jnp.int32, (shots, shots * steps), 0), 1.0, 0.0
    ).astype(BF16)
    wide = jnp.dot(signs.astype(BF16), spread, preferred_element_type=F32)
    wide = jnp.broadcast_to(wide[:, None, :], (n, 8, shots * steps))
    same_step = (
        lax.broadcasted_iota(jnp.int32, (n, 8, shots * steps), 2) & (steps - 1)
    ) == lax.broadcasted_iota(jnp.int32, (n, 8, shots * steps), 1)
    wide = jnp.where(same_step, wide, 0.0).reshape(n * 8, shots * steps).astype(BF16)
    loads[3].wait()
    traces = jnp.dot(
        wide, res_v[...].reshape(shots * steps, recvs), preferred_element_type=F32
    )
    part[...] = traces.reshape(n, 8, recvs)
    part[:, steps, pl.ds(0, shots)] = signs
    parts[e] = part[e]

    def enc_copy(k, incoming):
        to = lax.rem(e + k, n)
        slot = lax.rem(e - k + n, n) if incoming else e
        return pltpu.make_async_remote_copy(
            src_ref=part.at[to],
            dst_ref=parts.at[slot],
            send_sem=enc_send.at[k],
            recv_sem=enc_recv.at[k],
            device_id={"enc": to},
            device_id_type=MESH,
        )

    def enc_start(k, carry):
        enc_copy(k, False).start()
        return carry

    lax.fori_loop(1, n, enc_start, 0)

    across = lax.broadcasted_iota(jnp.int32, (2 * length, length), 0) & (length - 1)
    gap = jnp.abs(across - lax.broadcasted_iota(jnp.int32, (2 * length, length), 1))
    weight = jnp.zeros((2 * length, length), F32)
    for k in range(4):
        weight = jnp.where(gap == k + 1, RINGS[k], weight)
    band[...] = weight.astype(BF16)

    base = d * (depth * width * length)
    hot_rows = 4 * width
    hot_cols = 4 * length

    def row_of(cell):
        return (lax.shift_right_arithmetic(cell, shift + 9) << shift) | (
            lax.shift_right_arithmetic(cell, 7) & (width - 1)
        )

    def col_of(cell):
        return ((lax.shift_right_arithmetic(cell, shift + 7) & 3) << 7) | (cell & 127)

    def enc_wait(k, carry):
        enc_copy(k, True).wait_recv()
        return carry

    lax.fori_loop(1, n, enc_wait, 0)

    total = parts[0]
    for i in range(1, n):
        total = total + parts[i]
    total = total * (1.0 / (shots * n) ** 0.5)
    cell = receiver_pos[...] - base
    row_hot = jnp.where(
        lax.broadcasted_iota(jnp.int32, (hot_rows, recvs), 0) == row_of(cell), 1.0, 0.0
    ).astype(BF16)
    rows_hot[:, pl.ds(0, recvs)] = row_hot
    rows_hot[:, pl.ds(recvs, recvs)] = row_hot
    col_hit = lax.broadcasted_iota(jnp.int32, (hot_cols, recvs), 0) == col_of(cell)
    for t in range(steps):
        value = total[t : t + 1, :]
        high = value.astype(BF16).astype(F32)
        cols_hot[:, pl.ds(0, recvs)] = jnp.where(col_hit, high, 0.0).astype(BF16)
        cols_hot[:, pl.ds(recvs, recvs)] = jnp.where(col_hit, value - high, 0.0).astype(BF16)

        def receivers(q, carry):
            placed = lax.dot_general(
                rows_hot[pl.ds(pl.multiple_of(q * width, width), width), pl.ds(0, 2 * recvs)],
                cols_hot[:, pl.ds(0, 2 * recvs)],
                (((1,), (1,)), ((), ())),
                preferred_element_type=F32,
            )
            for r in range(4):
                inject[t, q * 4 + r] = placed[:, r * length : (r + 1) * length]
            return carry

        lax.fori_loop(0, 4, receivers, 0)

    group = 4

    def sources(g, carry):
        for i in range(group):
            at = g * group + i
            cell = source_pos[at] - base
            cols = pl.ds(i * shots, shots)
            rows_hot[:, cols] = jnp.where(
                lax.broadcasted_iota(jnp.int32, (hot_rows, shots), 0) == row_of(cell), 1.0, 0.0
            ).astype(BF16)
            sign = parts[at, steps : steps + 1, pl.ds(0, shots)]
            cols_hot[:, cols] = jnp.where(
                lax.broadcasted_iota(jnp.int32, (hot_cols, shots), 0) == col_of(cell), sign, 0.0
            ).astype(BF16)
        for q in range(4):
            placed = lax.dot_general(
                rows_hot[pl.ds(q * width, width), pl.ds(0, group * shots)],
                cols_hot[:, pl.ds(0, group * shots)],
                (((1,), (1,)), ((), ())),
                preferred_element_type=F32,
            )
            for r in range(4):
                pattern[q * 4 + r] += placed[:, r * length : (r + 1) * length]
        return carry

    pattern[...] = jnp.zeros(pattern.shape, F32)
    lax.fori_loop(0, n // group, sources, 0)

    def laplace(field, x0):
        column = field[:, pl.ds(pl.multiple_of(x0 + PAD, 8), 8), :]
        mid = column[HALO : HALO + depth]
        flat = mid.reshape(depth * 8, length)
        high = flat.astype(BF16)
        low = (flat - high.astype(F32)).astype(BF16)
        lanes = jnp.dot(
            jnp.concatenate([high, low], axis=1), band[...], preferred_element_type=F32
        ).reshape(depth, 8, length)
        total = CENTER * mid + lanes
        for k in range(4):
            near = column[HALO + 1 + k : HALO + 1 + k + depth] + column[3 - k : 3 - k + depth]
            near = near + field[inner, pl.ds(x0 + PAD + 1 + k, 8), :]
            near = near + field[inner, pl.ds(x0 + PAD - 1 - k, 8), :]
            total = total + RINGS[k] * near
        return mid, total

    def forward(t, now, prev):
        def tile(j, carry):
            x0 = pl.multiple_of(j * 8, 8)
            rows = pl.ds(x0, 8)
            padded = pl.ds(pl.multiple_of(x0 + PAD, 8), 8)
            mid, image = laplace(now, x0)
            prev[inner, padded, :] = (
                (mid + mid - prev[inner, padded, :])
                + cour_v[:, rows, :] * image
                + wavelet[t] * pattern[:, rows, :]
            )
            if t == 0:
                image_0[:, rows, :] = image
            elif t == 1:
                image_1[:, rows, :] = image
            elif t == 2:
                grad[:, rows, :] = image * a_4[:, rows, :]
            else:
                grad[:, rows, :] += image * a_5[:, rows, :]
            return carry

        lax.fori_loop(0, width // 8, tile, 0)

    def grad_copy(to, slot):
        return pltpu.make_async_remote_copy(
            src_ref=gsend.at[to],
            dst_ref=grecv.at[slot],
            send_sem=grad_send.at[to],
            recv_sem=grad_recv.at[slot],
            device_id={"enc": to},
            device_id_type=MESH,
        )

    def adjoint(t, w_now, w_next, now, later, new):
        def tile(i, carry):
            j = lax.rem(e + 1 + i, n) if t == 0 else i
            x0 = pl.multiple_of(j * 8, 8)
            rows = pl.ds(x0, 8)
            _, along = laplace(w_now, x0)
            value = now[:, rows, :]
            value = (value + value - later[:, rows, :]) + along + inject[t, :, rows, :]
            new[:, rows, :] = value
            if t > 0:
                w_next[inner, pl.ds(pl.multiple_of(x0 + PAD, 8), 8), :] = cour_v[:, rows, :] * value
            if t == 1:
                grad[:, rows, :] += value * image_1[:, rows, :]
            if t == 0:
                gsend[j] = grad[:, rows, :] + value * image_0[:, rows, :]

                @pl.when(j != e)
                def _():
                    grad_copy(j, e).start()

            return carry

        lax.fori_loop(0, width // 8, tile, 0)

    loads[0].wait()
    loads[4].wait()
    loads[5].wait()
    halo_wait(0, fwd_now, u_a)
    forward(0, u_a, u_b)
    halo_start(2, u_b, u_b)
    halo_wait(1, w_a, w_a)
    adjoint(3, w_a, w_b, a_4, a_5, a_5)
    halo_start(3, w_b, w_b)

    halo_wait(2, u_b, u_b)
    halo_sent(0, fwd_now, u_a)
    forward(1, u_b, u_a)
    halo_start(4, u_a, u_a)
    halo_wait(3, w_b, w_b)
    halo_sent(1, w_a, w_a)
    adjoint(2, w_b, w_a, a_5, a_4, a_4)
    halo_start(5, w_a, w_a)

    halo_wait(4, u_a, u_a)
    halo_sent(2, u_b, u_b)
    forward(2, u_a, u_b)
    halo_start(6, u_b, u_b)
    halo_wait(5, w_a, w_a)
    halo_sent(3, w_b, w_b)
    adjoint(1, w_a, w_b, a_4, a_5, a_1)
    halo_start(7, w_b, w_b)

    halo_wait(6, u_b, u_b)
    halo_sent(4, u_a, u_a)
    forward(3, u_b, u_a)
    store_u = pltpu.make_async_copy(u_a.at[inner, body_rows, :], fwd_last.at[0], store_sem.at[0])
    store_u.start()
    halo_wait(7, w_b, w_b)
    adjoint(0, w_b, None, a_1, a_4, a_4)
    store_a = pltpu.make_async_copy(a_4, adj_first.at[0], store_sem.at[1])
    store_a.start()

    def grad_wait(k, share):
        slot = lax.rem(e + k, n)
        grad_copy(slot, slot).wait_recv()
        return share + grecv[slot]

    share = lax.fori_loop(1, n, grad_wait, gsend[e])
    gout[...] = share * (1.0 / (UNIT * steps * n))
    store_g = pltpu.make_async_copy(gout, gradient, store_sem.at[2])
    store_g.start()

    def finish(k, carry):
        enc_copy(k, False).wait_send()
        to = lax.rem(e + k, n)
        grad_copy(to, to).wait_send()
        return carry

    lax.fori_loop(1, n, finish, 0)
    halo_sent(5, w_a, w_a)
    halo_sent(6, u_b, u_b)
    halo_sent(7, w_b, w_b)
    store_u.wait()
    store_a.wait()
    store_g.wait()


def body(
    n,
    nd,
    residual,
    weights,
    source_pos,
    receiver_pos,
    wavelet,
    courant,
    fwd_prev,
    fwd_now,
    adj_next,
    adj_now,
):
    shots, steps, recvs = residual.shape
    depth, width, length = courant.shape
    share = (depth, width // n, length)
    field = pltpu.VMEM((depth, width, length), F32)
    padded = pltpu.VMEM((depth + 2 * HALO, width + 2 * PAD, length), F32)
    hot = max(2 * recvs, 4 * shots)
    anywhere = pl.BlockSpec(memory_space=pl.ANY)
    vmem = pl.BlockSpec(memory_space=pltpu.VMEM)
    return pl.pallas_call(
        functools.partial(kernel, n, nd),
        out_shape=(
            jax.ShapeDtypeStruct(share, F32),
            jax.ShapeDtypeStruct((1, depth, width, length), F32),
            jax.ShapeDtypeStruct((1, depth, width, length), F32),
        ),
        in_specs=[
            anywhere,
            vmem,
            vmem,
            vmem,
            pl.BlockSpec(memory_space=pltpu.SMEM),
            anywhere,
            anywhere,
            anywhere,
            anywhere,
            anywhere,
        ],
        out_specs=(anywhere, anywhere, anywhere),
        scratch_shapes=[
            pltpu.VMEM((shots, steps, recvs), BF16),
            field,
            padded,
            padded,
            padded,
            padded,
            field,
            field,
            field,
            field,
            field,
            field,
            field,
            pltpu.VMEM((steps, depth, width, length), F32),
            pltpu.VMEM((2 * length, length), BF16),
            pltpu.VMEM((4 * width, hot), BF16),
            pltpu.VMEM((4 * length, hot), BF16),
            pltpu.VMEM((n, 8, recvs), F32),
            pltpu.VMEM((n, 8, recvs), F32),
            pltpu.VMEM((n,) + share, F32),
            pltpu.VMEM((n,) + share, F32),
            pltpu.VMEM(share, F32),
            pltpu.SemaphoreType.DMA((6,)),
            pltpu.SemaphoreType.DMA((3,)),
            pltpu.SemaphoreType.DMA((n,)),
            pltpu.SemaphoreType.DMA((n,)),
            pltpu.SemaphoreType.DMA((8, 2)),
            pltpu.SemaphoreType.DMA((8, 2)),
            pltpu.SemaphoreType.DMA((n,)),
            pltpu.SemaphoreType.DMA((n,)),
        ],
        compiler_params=pltpu.CompilerParams(
            collective_id=0, has_side_effects=True, vmem_limit_bytes=56 * 2**20
        ),
    )(
        residual,
        weights,
        source_pos.reshape(n, 1, shots),
        receiver_pos.reshape(1, recvs),
        wavelet,
        courant,
        fwd_prev,
        fwd_now,
        adj_next,
        adj_now,
    )


def solution(mesh):
    placed = (
        P("enc", None, "dom"),
        P(None, "enc"),
        P(),
        P("dom"),
        P(),
        P("dom", None, None),
        P("enc", "dom", None, None),
        P("enc", "dom", None, None),
        P("enc", "dom", None, None),
        P("enc", "dom", None, None),
    )
    return jax.shard_map(
        functools.partial(body, mesh.shape["enc"], mesh.shape["dom"]),
        mesh=mesh,
        in_specs=placed,
        out_specs=(P("dom", "enc", None), P("enc", "dom", None, None), P("enc", "dom", None, None)),
        check_vma=False,
    )
```

profile of v0, /device:TPU:128, one launch (start us, length us, event | category | flops | bytes accessed | tf_op | source)
XLA Modules:
  0.0 79.5 jit_solution(6304987754988876882)
XLA Ops:
  0.6 74.0 %shard_map.121 = (f32[16,8,128]{2,1,0:T(8,128)}, f32[1,16,128,128]{3,2,1,0:T(8,128)}, f32[1,16,128,128]{3,2,1,0:T(8,128)}) custom-call(bf16[256,4,512]{2,1,0:T(4,128)(2,1)} %residual.1, s32[16,256]{1,0:T(8,128)} %weights.1, s32[16,1,256]{2,1,0:T(1,128)} %bitcast.2, s32[1,512]{1,0:T(1,128)} %bitcast.3, f32[4]{0:T(128)} %wavelet.1, f32[16,128,128]{2,1,0:T(8,128)} %courant.1, ...), custom_call_target="tpu_custom_call" | custom-call | tf_op jit(solution)/shard_map/pallas_call | solution.py:461
  74.7 1.5 %copy.16 = f32[16,8,128]{2,1,0:T(8,128)} copy(f32[16,8,128]{2,1,0:T(8,128)} %get-tuple-element.6) | data formatting | bytes 131072
  76.1 0.0 copy-start
  76.1 2.4 %copy.17 = f32[1,16,128,128]{3,2,1,0:T(8,128)} copy(f32[1,16,128,128]{3,2,1,0:T(8,128)} %get-tuple-element.7) | data formatting | bytes 2097152
  78.5 0.0 copy-done
  78.5 1.0 %copy.18 = f32[1,16,128,128]{3,2,1,0:T(8,128)} copy(f32[1,16,128,128]{3,2,1,0:T(8,128)S(1)} %copy-done) | data formatting | bytes 2097152
Async XLA Ops:
  76.1 2.4 %copy-start = (f32[1,16,128,128]{3,2,1,0:T(8,128)S(1)}, f32[1,16,128,128]{3,2,1,0:T(8,128)}, u32[]{:S(2)}) copy-start(f32[1,16,128,128]{3,2,1,0:T(8,128)} %get-tuple-element.8) | copy-start | bytes 3145732
where the time goes:
time: 80 us; the launch traced here: 79.5 us
  Pallas kernels  74 us (92%)
  local copies, waits for them, and re-layouts  4.83 us (6%)
    pallas_call x1, Pallas kernels, body(): pl.pallas_call(functools.partial(kernel, n, nd), out_shape=(jax.ShapeDtyp...  74 us
    unnamed x5, local copies, waits for them, and re-layouts  4.83 us

commit v1 on v0

--- a/solution.py
+++ b/solution.py
@@ -15,6 +15,9 @@
 RINGS = (8064.0, -1008.0, 128.0, -9.0)
 PAD = 8
 HALO = 4
+TILE = 16
+UNROLL = 4
+LAST_UNROLL = 4
 
 
 def kernel(
@@ -48,10 +51,12 @@
     pattern,
     inject,
     band,
-    rows_hot,
+    src_rows,
+    recv_rows,
     cols_hot,
     part,
     parts,
+    traces_v,
     gsend,
     grecv,
     gout,
@@ -85,19 +90,6 @@
     for copy in loads:
         copy.start()
 
-    for field in (u_a, u_b, w_a, w_b):
-        edge = jnp.zeros((depth + 2 * HALO, PAD, length), F32)
-        field[:, pl.ds(0, PAD), :] = edge
-        field[:, pl.ds(PAD + width, PAD), :] = edge
-
-        @pl.when(d == 0)
-        def _():
-            field[pl.ds(0, HALO)] = jnp.zeros((HALO, width + 2 * PAD, length), F32)
-
-        @pl.when(d == nd - 1)
-        def _():
-            field[pl.ds(HALO + depth, HALO)] = jnp.zeros((HALO, width + 2 * PAD, length), F32)
-
     barrier = pltpu.get_barrier_semaphore()
 
     def greet(k, carry):
@@ -115,6 +107,31 @@
     @pl.when(d < nd - 1)
     def _():
         pl.semaphore_signal(barrier, inc=1, device_id={"dom": d + 1}, device_id_type=MESH)
+
+    for field in (u_a, u_b, w_a, w_b):
+        edge = jnp.zeros((depth + 2 * HALO, PAD, length), F32)
+        field[:, pl.ds(0, PAD), :] = edge
+        field[:, pl.ds(PAD + width, PAD), :] = edge
+
+        @pl.when(d == 0)
+        def _():
+            field[pl.ds(0, HALO)] = jnp.zeros((HALO, width + 2 * PAD, length), F32)
+
+        @pl.when(d == nd - 1)
+        def _():
+            field[pl.ds(HALO + depth, HALO)] = jnp.zeros((HALO, width + 2 * PAD, length), F32)
+
+    loads[1].wait()
+    loads[2].wait()
+
+    def scale_tile(j, carry):
+        rows = pl.ds(pl.multiple_of(j * 8, 8), 8)
+        scaled = cour_v[:, rows, :] * (1.0 / UNIT)
+        cour_v[:, rows, :] = scaled
+        w_a[inner, pl.ds(pl.multiple_of(j * 8 + PAD, 8), 8), :] = scaled * a_4[:, rows, :]
+        return carry
+
+    lax.fori_loop(0, width // 8, scale_tile, 0)
 
     pl.semaphore_wait(
         barrier, n - 1 + (d > 0).astype(jnp.int32) + (d < nd - 1).astype(jnp.int32)
@@ -165,18 +182,6 @@
             halo_copy(h, source, field, False).wait_recv()
 
     halo_start(0, fwd_now, u_a)
-
-    loads[1].wait()
-    loads[2].wait()
-
-    def scale_tile(j, carry):
-        rows = pl.ds(pl.multiple_of(j * 8, 8), 8)
-        scaled = cour_v[:, rows, :] * (1.0 / UNIT)
-        cour_v[:, rows, :] = scaled
-        w_a[inner, pl.ds(pl.multiple_of(j * 8 + PAD, 8), 8), :] = scaled * a_4[:, rows, :]
-        return carry
-
-    lax.fori_loop(0, width // 8, scale_tile, 0)
     halo_start(1, w_a, w_a)
 
     signs = weights[...].astype(F32)
@@ -239,192 +244,267 @@
         enc_copy(k, True).wait_recv()
         return carry
 
-    lax.fori_loop(1, n, enc_wait, 0)
-
-    total = parts[0]
-    for i in range(1, n):
-        total = total + parts[i]
-    total = total * (1.0 / (shots * n) ** 0.5)
-    cell = receiver_pos[...] - base
+    group = 4
+
+    def source_rows(g, carry):
+        for i in range(group):
+            cell = source_pos[g * group + i] - base
+            src_rows[g, :, pl.ds(i * shots, shots)] = jnp.where(
+                lax.broadcasted_iota(jnp.int32, (hot_rows, shots), 0) == row_of(cell), 1.0, 0.0
+            ).astype(BF16)
+        return carry
+
+    lax.fori_loop(0, n // group, source_rows, 0)
+    recv_cell = receiver_pos[...] - base
     row_hot = jnp.where(
-        lax.broadcasted_iota(jnp.int32, (hot_rows, recvs), 0) == row_of(cell), 1.0, 0.0
+        lax.broadcasted_iota(jnp.int32, (hot_rows, recvs), 0) == row_of(recv_cell), 1.0, 0.0
     ).astype(BF16)
-    rows_hot[:, pl.ds(0, recvs)] = row_hot
-    rows_hot[:, pl.ds(recvs, recvs)] = row_hot
-    col_hit = lax.broadcasted_iota(jnp.int32, (hot_cols, recvs), 0) == col_of(cell)
-    for t in range(steps):
-        value = total[t : t + 1, :]
-        high = value.astype(BF16).astype(F32)
-        cols_hot[:, pl.ds(0, recvs)] = jnp.where(col_hit, high, 0.0).astype(BF16)
-        cols_hot[:, pl.ds(recvs, recvs)] = jnp.where(col_hit, value - high, 0.0).astype(BF16)
-
-        def receivers(q, carry):
-            placed = lax.dot_general(
-                rows_hot[pl.ds(pl.multiple_of(q * width, width), width), pl.ds(0, 2 * recvs)],
-                cols_hot[:, pl.ds(0, 2 * recvs)],
-                (((1,), (1,)), ((), ())),
-                preferred_element_type=F32,
-            )
-            for r in range(4):
-                inject[t, q * 4 + r] = placed[:, r * length : (r + 1) * length]
-            return carry
-
-        lax.fori_loop(0, 4, receivers, 0)
-
-    group = 4
+    recv_rows[:, pl.ds(0, recvs)] = row_hot
+    recv_rows[:, pl.ds(recvs, recvs)] = row_hot
+
+    def spread_out(rows, cols):
+        return lax.dot_general(
+            rows, cols, (((1,), (1,)), ((), ())), preferred_element_type=F32
+        )
 
     def sources(g, carry):
         for i in range(group):
             at = g * group + i
             cell = source_pos[at] - base
-            cols = pl.ds(i * shots, shots)
-            rows_hot[:, cols] = jnp.where(
-                lax.broadcasted_iota(jnp.int32, (hot_rows, shots), 0) == row_of(cell), 1.0, 0.0
-            ).astype(BF16)
             sign = parts[at, steps : steps + 1, pl.ds(0, shots)]
-            cols_hot[:, cols] = jnp.where(
+            cols_hot[:, pl.ds(i * shots, shots)] = jnp.where(
                 lax.broadcasted_iota(jnp.int32, (hot_cols, shots), 0) == col_of(cell), sign, 0.0
             ).astype(BF16)
+        placed = spread_out(src_rows[g], cols_hot[:, pl.ds(0, group * shots)])
         for q in range(4):
-            placed = lax.dot_general(
-                rows_hot[pl.ds(q * width, width), pl.ds(0, group * shots)],
-                cols_hot[:, pl.ds(0, group * shots)],
-                (((1,), (1,)), ((), ())),
-                preferred_element_type=F32,
-            )
             for r in range(4):
-                pattern[q * 4 + r] += placed[:, r * length : (r + 1) * length]
+                pattern[q * 4 + r] += placed[
+                    q * width : (q + 1) * width, r * length : (r + 1) * length
+                ]
         return carry
 
-    pattern[...] = jnp.zeros(pattern.shape, F32)
-    lax.fori_loop(0, n // group, sources, 0)
-
-    def laplace(field, x0):
-        column = field[:, pl.ds(pl.multiple_of(x0 + PAD, 8), 8), :]
-        mid = column[HALO : HALO + depth]
-        flat = mid.reshape(depth * 8, length)
+    def receivers(t):
+        value = traces_v[t : t + 1, :]
+        high = value.astype(BF16).astype(F32)
+        hit = lax.broadcasted_iota(jnp.int32, (hot_cols, recvs), 0) == col_of(recv_cell)
+        cols_hot[:, pl.ds(0, recvs)] = jnp.where(hit, high, 0.0).astype(BF16)
+        cols_hot[:, pl.ds(recvs, recvs)] = jnp.where(hit, value - high, 0.0).astype(BF16)
+        placed = spread_out(recv_rows[...], cols_hot[:, pl.ds(0, 2 * recvs)])
+        for q in range(4):
+            for r in range(4):
+                inject[t, q * 4 + r] = placed[
+                    q * width : (q + 1) * width, r * length : (r + 1) * length
+                ]
+
+    def laplace(field, z0, nz, x0, nx):
+        column = field[pl.ds(z0, nz + 2 * HALO), pl.ds(pl.multiple_of(x0 + PAD, 8), nx), :]
+        mid = column[HALO : HALO + nz]
+        flat = mid.reshape(nz * nx, length)
         high = flat.astype(BF16)
         low = (flat - high.astype(F32)).astype(BF16)
         lanes = jnp.dot(
             jnp.concatenate([high, low], axis=1), band[...], preferred_element_type=F32
-        ).reshape(depth, 8, length)
+        ).reshape(nz, nx, length)
         total = CENTER * mid + lanes
+        planes = pl.ds(z0 + HALO, nz)
         for k in range(4):
-            near = column[HALO + 1 + k : HALO + 1 + k + depth] + column[3 - k : 3 - k + depth]
-            near = near + field[inner, pl.ds(x0 + PAD + 1 + k, 8), :]
-            near = near + field[inner, pl.ds(x0 + PAD - 1 - k, 8), :]
+            near = column[HALO + 1 + k : HALO + 1 + k + nz] + column[3 - k : 3 - k + nz]
+            near = near + field[planes, pl.ds(x0 + PAD + 1 + k, nx), :]
+            near = near + field[planes, pl.ds(x0 + PAD - 1 - k, nx), :]
             total = total + RINGS[k] * near
         return mid, total
 
+    faces = ((0, HALO), (depth - HALO, HALO))
+    middle = ((HALO, depth - 2 * HALO),)
+
+    def sweep(blocks, work, unroll=UNROLL):
+        def tile(j, carry):
+            x0 = pl.multiple_of(j * TILE, TILE)
+            for z0, nz in blocks:
+                work(z0, nz, x0)
+            return carry
+
+        lax.fori_loop(0, width // TILE, tile, 0, unroll=unroll)
+
     def forward(t, now, prev):
-        def tile(j, carry):
-            x0 = pl.multiple_of(j * 8, 8)
-            rows = pl.ds(x0, 8)
-            padded = pl.ds(pl.multiple_of(x0 + PAD, 8), 8)
-            mid, image = laplace(now, x0)
-            prev[inner, padded, :] = (
-                (mid + mid - prev[inner, padded, :])
-                + cour_v[:, rows, :] * image
-                + wavelet[t] * pattern[:, rows, :]
-            )
+        def work(z0, nz, x0):
+            planes = pl.ds(z0, nz)
+            rows = pl.ds(x0, TILE)
+            at = (pl.ds(z0 + HALO, nz), pl.ds(pl.multiple_of(x0 + PAD, 8), TILE))
+            mid, image = laplace(now, z0, nz, x0, TILE)
+            value = (mid + mid - prev[at]) + cour_v[planes, rows] * image
+            if t > 0:
+                value = value + wavelet[t] * pattern[planes, rows]
+            prev[at] = value
             if t == 0:
-                image_0[:, rows, :] = image
+                image_0[planes, rows] = image
             elif t == 1:
-                image_1[:, rows, :] = image
+                image_1[planes, rows] = image
             elif t == 2:
-                grad[:, rows, :] = image * a_4[:, rows, :]
+                grad[planes, rows] = image * a_4[planes, rows]
             else:
-                grad[:, rows, :] += image * a_5[:, rows, :]
-            return carry
-
-        lax.fori_loop(0, width // 8, tile, 0)
-
-    def grad_copy(to, slot):
+                grad[planes, rows] += image * a_5[planes, rows]
+
+        return work
+
+    def add_pattern(z0, nz, x0):
+        at = (pl.ds(z0 + HALO, nz), pl.ds(pl.multiple_of(x0 + PAD, 8), TILE))
+        u_b[at] += wavelet[0] * pattern[pl.ds(z0, nz), pl.ds(x0, TILE)]
+
+    def adjoint(t, w_now, w_next, now, later, new):
+        def work(z0, nz, x0):
+            planes = pl.ds(z0, nz)
+            rows = pl.ds(x0, TILE)
+            _, along = laplace(w_now, z0, nz, x0, TILE)
+            value = now[planes, rows]
+            value = (value + value - later[planes, rows]) + along
+            if t < steps - 1:
+                value = value + inject[t, planes, rows]
+                at = (pl.ds(z0 + HALO, nz), pl.ds(pl.multiple_of(x0 + PAD, 8), TILE))
+                w_next[at] = cour_v[planes, rows] * value
+            new[planes, rows] = value
+            if t == 1:
+                grad[planes, rows] += value * image_1[planes, rows]
+
+        return work
+
+    def add_inject(z0, nz, x0):
+        planes = pl.ds(z0, nz)
+        rows = pl.ds(x0, TILE)
+        at = (pl.ds(z0 + HALO, nz), pl.ds(pl.multiple_of(x0 + PAD, 8), TILE))
+        value = a_5[planes, rows] + inject[steps - 1, planes, rows]
+        a_5[planes, rows] = value
+        w_b[at] = cour_v[planes, rows] * value
+
+    half = depth // 2
+
+    def grad_copy(to, slot, part_no):
         return pltpu.make_async_remote_copy(
-            src_ref=gsend.at[to],
-            dst_ref=grecv.at[slot],
-            send_sem=grad_send.at[to],
-            recv_sem=grad_recv.at[slot],
+            src_ref=gsend.at[part_no, to],
+            dst_ref=grecv.at[part_no, slot],
+            send_sem=grad_send.at[part_no, to],
+            recv_sem=grad_recv.at[part_no, slot],
             device_id={"enc": to},
             device_id_type=MESH,
         )
 
-    def adjoint(t, w_now, w_next, now, later, new):
+    def last_adjoint(part_no, blocks):
         def tile(i, carry):
-            j = lax.rem(e + 1 + i, n) if t == 0 else i
+            j = lax.rem(e + 1 + i, n)
             x0 = pl.multiple_of(j * 8, 8)
             rows = pl.ds(x0, 8)
-            _, along = laplace(w_now, x0)
-            value = now[:, rows, :]
-            value = (value + value - later[:, rows, :]) + along + inject[t, :, rows, :]
-            new[:, rows, :] = value
-            if t > 0:
-                w_next[inner, pl.ds(pl.multiple_of(x0 + PAD, 8), 8), :] = cour_v[:, rows, :] * value
-            if t == 1:
-                grad[:, rows, :] += value * image_1[:, rows, :]
-            if t == 0:
-                gsend[j] = grad[:, rows, :] + value * image_0[:, rows, :]
-
-                @pl.when(j != e)
-                def _():
-                    grad_copy(j, e).start()
+            put = 0
+            for z0, nz in blocks:
+                planes = pl.ds(z0, nz)
+                _, along = laplace(w_b, z0, nz, x0, 8)
+                value = a_1[planes, rows]
+                value = (value + value - a_4[planes, rows]) + along + inject[0, planes, rows]
+                a_4[planes, rows] = value
+                gsend[part_no, j, pl.ds(put, nz)] = (
+                    grad[planes, rows] + value * image_0[planes, rows]
+                )
+                put += nz
+
+            @pl.when(j != e)
+            def _():
+                grad_copy(j, e, part_no).start()
 
             return carry
 
-        lax.fori_loop(0, width // 8, tile, 0)
+        lax.fori_loop(0, n, tile, 0, unroll=LAST_UNROLL)
 
     loads[0].wait()
     loads[4].wait()
     loads[5].wait()
+    work = forward(0, u_a, u_b)
+    sweep(middle, work)
     halo_wait(0, fwd_now, u_a)
-    forward(0, u_a, u_b)
+    sweep(faces, work)
+    work = adjoint(3, w_a, w_b, a_4, a_5, a_5)
+    sweep(middle, work)
+    halo_wait(1, w_a, w_a)
+    sweep(faces, work)
+
+    lax.fori_loop(1, n, enc_wait, 0)
+    pattern[...] = jnp.zeros(pattern.shape, F32)
+    lax.fori_loop(0, n // group, sources, 0)
+    sweep(faces, add_pattern)
     halo_start(2, u_b, u_b)
-    halo_wait(1, w_a, w_a)
-    adjoint(3, w_a, w_b, a_4, a_5, a_5)
+    sweep(middle, add_pattern)
+
+    total = parts[0]
+    for i in range(1, n):
+        total = total + parts[i]
+    traces_v[...] = total * (1.0 / (shots * n) ** 0.5)
+    receivers(3)
+    sweep(faces, add_inject)
     halo_start(3, w_b, w_b)
-
+    sweep(middle, add_inject)
+    for t in range(3):
+        receivers(2 - t)
+
+    halo_sent(0, fwd_now, u_a)
+    work = forward(1, u_b, u_a)
     halo_wait(2, u_b, u_b)
-    halo_sent(0, fwd_now, u_a)
-    forward(1, u_b, u_a)
+    sweep(faces, work)
     halo_start(4, u_a, u_a)
+    sweep(middle, work)
+
+    halo_sent(1, w_a, w_a)
+    work = adjoint(2, w_b, w_a, a_5, a_4, a_4)
     halo_wait(3, w_b, w_b)
-    halo_sent(1, w_a, w_a)
-    adjoint(2, w_b, w_a, a_5, a_4, a_4)
+    sweep(faces, work)
     halo_start(5, w_a, w_a)
-
+    sweep(middle, work)
+
+    halo_sent(2, u_b, u_b)
+    work = forward(2, u_a, u_b)
     halo_wait(4, u_a, u_a)
-    halo_sent(2, u_b, u_b)
-    forward(2, u_a, u_b)
+    sweep(faces, work)
     halo_start(6, u_b, u_b)
+    sweep(middle, work)
+
+    halo_sent(3, w_b, w_b)
+    work = adjoint(1, w_a, w_b, a_4, a_5, a_1)
     halo_wait(5, w_a, w_a)
-    halo_sent(3, w_b, w_b)
-    adjoint(1, w_a, w_b, a_4, a_5, a_1)
+    sweep(faces, work)
     halo_start(7, w_b, w_b)
-
+    sweep(middle, work)
+
+    halo_sent(4, u_a, u_a)
+    work = forward(3, u_b, u_a)
+    sweep(middle, work)
     halo_wait(6, u_b, u_b)
-    halo_sent(4, u_a, u_a)
-    forward(3, u_b, u_a)
+    sweep(faces, work)
     store_u = pltpu.make_async_copy(u_a.at[inner, body_rows, :], fwd_last.at[0], store_sem.at[0])
     store_u.start()
+
+    last_adjoint(0, middle)
     halo_wait(7, w_b, w_b)
-    adjoint(0, w_b, None, a_1, a_4, a_4)
+    last_adjoint(1, faces)
     store_a = pltpu.make_async_copy(a_4, adj_first.at[0], store_sem.at[1])
     store_a.start()
 
-    def grad_wait(k, share):
-        slot = lax.rem(e + k, n)
-        grad_copy(slot, slot).wait_recv()
-        return share + grecv[slot]
-
-    share = lax.fori_loop(1, n, grad_wait, gsend[e])
-    gout[...] = share * (1.0 / (UNIT * steps * n))
+    def grad_sum(part_no):
+        def grad_wait(k, share):
+            slot = lax.rem(e + k, n)
+            grad_copy(slot, slot, part_no).wait_recv()
+            return share + grecv[part_no, slot]
+
+        return lax.fori_loop(1, n, grad_wait, gsend[part_no, e]) * (1.0 / (UNIT * steps * n))
+
+    gout[pl.ds(HALO, half)] = grad_sum(0)
+    share = grad_sum(1)
+    gout[pl.ds(0, HALO)] = share[:HALO]
+    gout[pl.ds(depth - HALO, HALO)] = share[HALO:]
     store_g = pltpu.make_async_copy(gout, gradient, store_sem.at[2])
     store_g.start()
 
     def finish(k, carry):
         enc_copy(k, False).wait_send()
         to = lax.rem(e + k, n)
-        grad_copy(to, to).wait_send()
+        grad_copy(to, to, 0).wait_send()
+        grad_copy(to, to, 1).wait_send()
         return carry
 
     lax.fori_loop(1, n, finish, 0)
@@ -494,12 +574,14 @@
             field,
             pltpu.VMEM((steps, depth, width, length), F32),
             pltpu.VMEM((2 * length, length), BF16),
-            pltpu.VMEM((4 * width, hot), BF16),
+            pltpu.VMEM((n // 4, 4 * width, 4 * shots), BF16),
+            pltpu.VMEM((4 * width, 2 * recvs), BF16),
             pltpu.VMEM((4 * length, hot), BF16),
             pltpu.VMEM((n, 8, recvs), F32),
             pltpu.VMEM((n, 8, recvs), F32),
-            pltpu.VMEM((n,) + share, F32),
-            pltpu.VMEM((n,) + share, F32),
+            pltpu.VMEM((8, recvs), F32),
+            pltpu.VMEM((2, n, depth // 2) + share[1:], F32),
+            pltpu.VMEM((2, n, depth // 2) + share[1:], F32),
             pltpu.VMEM(share, F32),
             pltpu.SemaphoreType.DMA((6,)),
             pltpu.SemaphoreType.DMA((3,)),
@@ -507,8 +589,8 @@
             pltpu.SemaphoreType.DMA((n,)),
             pltpu.SemaphoreType.DMA((8, 2)),
             pltpu.SemaphoreType.DMA((8, 2)),
-            pltpu.SemaphoreType.DMA((n,)),
-            pltpu.SemaphoreType.DMA((n,)),
+            pltpu.SemaphoreType.DMA((2, n)),
+            pltpu.SemaphoreType.DMA((2, n)),
         ],
         compiler_params=pltpu.CompilerParams(
             collective_id=0, has_side_effects=True, vmem_limit_bytes=56 * 2**20

time: 80 us -> 59 us (0.74)
  Pallas kernels: 74 us -> 52.6 us
    pallas_call x1, Pallas kernels: 74 us -> 52.6 us  [body(): pl.pallas_call(functools.partial(kernel, n, nd), out_shape=(jax.ShapeDtyp...]
where the time goes in v1:
time: 59 us; the launch traced here: 58.1 us
  Pallas kernels  52.6 us (89%)
  local copies, waits for them, and re-layouts  4.83 us (8%)
  between operations  0.64 us (1%)
    pallas_call x1, Pallas kernels, body(): pl.pallas_call(functools.partial(kernel, n, nd), out_shape=(jax.ShapeDtyp...  52.6 us
    unnamed x5, local copies, waits for them, and re-layouts  4.83 us

profile of v1, /device:TPU:128, one launch (start us, length us, event | category | flops | bytes accessed | tf_op | source)
XLA Modules:
  0.0 58.1 jit_solution(6362152027301729646)
XLA Ops:
  0.6 52.6 %shard_map.121 = (f32[16,8,128]{2,1,0:T(8,128)}, f32[1,16,128,128]{3,2,1,0:T(8,128)}, f32[1,16,128,128]{3,2,1,0:T(8,128)}) custom-call(bf16[256,4,512]{2,1,0:T(4,128)(2,1)} %residual.1, s32[16,256]{1,0:T(8,128)} %weights.1, s32[16,1,256]{2,1,0:T(1,128)} %bitcast.2, s32[1,512]{1,0:T(1,128)} %bitcast.3, f32[4]{0:T(128)} %wavelet.1, f32[16,128,128]{2,1,0:T(8,128)} %courant.1, ...), custom_call_target="tpu_custom_call" | custom-call | tf_op jit(solution)/shard_map/pallas_call | solution.py:541
  53.3 1.5 %copy.16 = f32[16,8,128]{2,1,0:T(8,128)} copy(f32[16,8,128]{2,1,0:T(8,128)} %get-tuple-element.6) | data formatting | bytes 131072
  54.7 0.0 copy-start
  54.7 2.4 %copy.17 = f32[1,16,128,128]{3,2,1,0:T(8,128)} copy(f32[1,16,128,128]{3,2,1,0:T(8,128)} %get-tuple-element.7) | data formatting | bytes 2097152
  57.1 0.0 copy-done
  57.1 1.0 %copy.18 = f32[1,16,128,128]{3,2,1,0:T(8,128)} copy(f32[1,16,128,128]{3,2,1,0:T(8,128)S(1)} %copy-done) | data formatting | bytes 2097152
Async XLA Ops:
  54.7 2.4 %copy-start = (f32[1,16,128,128]{3,2,1,0:T(8,128)S(1)}, f32[1,16,128,128]{3,2,1,0:T(8,128)}, u32[]{:S(2)}) copy-start(f32[1,16,128,128]{3,2,1,0:T(8,128)} %get-tuple-element.8) | copy-start | bytes 3145732

commit v2 on v1

--- a/solution.py
+++ b/solution.py
@@ -58,16 +58,24 @@
     parts,
     traces_v,
     gsend,
-    grecv,
-    gout,
+    gfirst,
+    gsum,
+    glast,
+    fsend,
+    frecv,
+    staged,
+    landed,
     load_sem,
-    store_sem,
     enc_send,
     enc_recv,
     halo_send,
     halo_recv,
-    grad_send,
-    grad_recv,
+    first_send,
+    first_recv,
+    last_send,
+    last_recv,
+    face_send,
+    face_recv,
 ):
     depth, width, length = cour_v.shape
     shots = weights.shape[1]
@@ -133,56 +141,81 @@
 
     lax.fori_loop(0, width // 8, scale_tile, 0)
 
+    def halo_copies(h, field, down):
+        way = 0 if down else 1
+        to = {"dom": d - 1 if down else d + 1}
+        face = field.at[HALO if down else HALO + depth - 1, body_rows, :]
+        land = field.at[HALO + depth if down else HALO - 1, body_rows, :]
+        return (
+            pltpu.make_async_remote_copy(
+                src_ref=face,
+                dst_ref=land,
+                send_sem=halo_send.at[h, way, 0],
+                recv_sem=halo_recv.at[h, way, 0],
+                device_id=to,
+                device_id_type=MESH,
+            ),
+            pltpu.make_async_remote_copy(
+                src_ref=staged.at[h, way],
+                dst_ref=landed.at[h, way],
+                send_sem=halo_send.at[h, way, 1],
+                recv_sem=halo_recv.at[h, way, 1],
+                device_id=to,
+                device_id_type=MESH,
+            ),
+        )
+
+    def halo_stage(h, field):
+        staged[h, 0] = field[pl.ds(HALO + 1, HALO - 1), body_rows, :].astype(BF16)
+        staged[h, 1] = field[pl.ds(depth, HALO - 1), body_rows, :].astype(BF16)
+
+    def halo_start(h, field, stage=True):
+        if stage:
+            halo_stage(h, field)
+
+        @pl.when(d > 0)
+        def _():
+            for copy in halo_copies(h, field, True):
+                copy.start()
+
+        @pl.when(d < nd - 1)
+        def _():
+            for copy in halo_copies(h, field, False):
+                copy.start()
+
+    def halo_sent(h, field):
+        @pl.when(d > 0)
+        def _():
+            for copy in halo_copies(h, field, True):
+                copy.wait_send()
+
+        @pl.when(d < nd - 1)
+        def _():
+            for copy in halo_copies(h, field, False):
+                copy.wait_send()
+
+    def halo_wait(h, field):
+        @pl.when(d < nd - 1)
+        def _():
+            for copy in halo_copies(h, field, True):
+                copy.wait_recv()
+            field[pl.ds(HALO + depth + 1, HALO - 1), body_rows, :] = landed[h, 0].astype(F32)
+
+        @pl.when(d > 0)
+        def _():
+            for copy in halo_copies(h, field, False):
+                copy.wait_recv()
+            field[pl.ds(0, HALO - 1), body_rows, :] = landed[h, 1].astype(F32)
+
+    loads[0].wait()
+    halo_stage(0, u_a)
+    halo_stage(1, w_a)
     pl.semaphore_wait(
         barrier, n - 1 + (d > 0).astype(jnp.int32) + (d < nd - 1).astype(jnp.int32)
     )
 
-    def halo_copy(h, source, field, down):
-        near = 0 if down else depth - HALO
-        if source is field:
-            src = field.at[pl.ds(HALO + near, HALO), body_rows, :]
-        else:
-            src = source.at[0, pl.ds(near, HALO)]
-        far = HALO + depth if down else 0
-        way = 0 if down else 1
-        return pltpu.make_async_remote_copy(
-            src_ref=src,
-            dst_ref=field.at[pl.ds(far, HALO), body_rows, :],
-            send_sem=halo_send.at[h, way],
-            recv_sem=halo_recv.at[h, way],
-            device_id={"dom": d - 1 if down else d + 1},
-            device_id_type=MESH,
-        )
-
-    def halo_start(h, source, field):
-        @pl.when(d > 0)
-        def _():
-            halo_copy(h, source, field, True).start()
-
-        @pl.when(d < nd - 1)
-        def _():
-            halo_copy(h, source, field, False).start()
-
-    def halo_sent(h, source, field):
-        @pl.when(d > 0)
-        def _():
-            halo_copy(h, source, field, True).wait_send()
-
-        @pl.when(d < nd - 1)
-        def _():
-            halo_copy(h, source, field, False).wait_send()
-
-    def halo_wait(h, source, field):
-        @pl.when(d < nd - 1)
-        def _():
-            halo_copy(h, source, field, True).wait_recv()
-
-        @pl.when(d > 0)
-        def _():
-            halo_copy(h, source, field, False).wait_recv()
-
-    halo_start(0, fwd_now, u_a)
-    halo_start(1, w_a, w_a)
+    halo_start(0, u_a, False)
+    halo_start(1, w_a, False)
 
     signs = weights[...].astype(F32)
     shot_of = lax.shift_right_logical(lax.broadcasted_iota(jnp.int32, (shots, shots * steps), 1), 2)
@@ -244,17 +277,14 @@
         enc_copy(k, True).wait_recv()
         return carry
 
-    group = 4
-
-    def source_rows(g, carry):
-        for i in range(group):
-            cell = source_pos[g * group + i] - base
-            src_rows[g, :, pl.ds(i * shots, shots)] = jnp.where(
-                lax.broadcasted_iota(jnp.int32, (hot_rows, shots), 0) == row_of(cell), 1.0, 0.0
-            ).astype(BF16)
+    def source_rows(i, carry):
+        cell = source_pos[i] - base
+        src_rows[:, pl.ds(pl.multiple_of(i * shots, shots), shots)] = jnp.where(
+            lax.broadcasted_iota(jnp.int32, (hot_rows, shots), 0) == row_of(cell), 1.0, 0.0
+        ).astype(BF16)
         return carry
 
-    lax.fori_loop(0, n // group, source_rows, 0)
+    lax.fori_loop(0, n, source_rows, 0)
     recv_cell = receiver_pos[...] - base
     row_hot = jnp.where(
         lax.broadcasted_iota(jnp.int32, (hot_rows, recvs), 0) == row_of(recv_cell), 1.0, 0.0
@@ -267,21 +297,22 @@
             rows, cols, (((1,), (1,)), ((), ())), preferred_element_type=F32
         )
 
-    def sources(g, carry):
-        for i in range(group):
-            at = g * group + i
-            cell = source_pos[at] - base
-            sign = parts[at, steps : steps + 1, pl.ds(0, shots)]
-            cols_hot[:, pl.ds(i * shots, shots)] = jnp.where(
-                lax.broadcasted_iota(jnp.int32, (hot_cols, shots), 0) == col_of(cell), sign, 0.0
-            ).astype(BF16)
-        placed = spread_out(src_rows[g], cols_hot[:, pl.ds(0, group * shots)])
+    def source_cols(i, carry):
+        cell = source_pos[i] - base
+        sign = parts[i, steps : steps + 1, pl.ds(0, shots)]
+        cols_hot[:, pl.ds(pl.multiple_of(i * shots, shots), shots)] = jnp.where(
+            lax.broadcasted_iota(jnp.int32, (hot_cols, shots), 0) == col_of(cell), sign, 0.0
+        ).astype(BF16)
+        return carry
+
+    def sources():
+        lax.fori_loop(0, n, source_cols, 0)
+        placed = spread_out(src_rows[...], cols_hot[:, pl.ds(0, n * shots)])
         for q in range(4):
             for r in range(4):
-                pattern[q * 4 + r] += placed[
+                pattern[q * 4 + r] = placed[
                     q * width : (q + 1) * width, r * length : (r + 1) * length
                 ]
-        return carry
 
     def receivers(t):
         value = traces_v[t : t + 1, :]
@@ -335,7 +366,10 @@
             value = (mid + mid - prev[at]) + cour_v[planes, rows] * image
             if t > 0:
                 value = value + wavelet[t] * pattern[planes, rows]
-            prev[at] = value
+            if t < steps - 1:
+                prev[at] = value
+            else:
+                fwd_last[0, planes, rows] = value
             if t == 0:
                 image_0[planes, rows] = image
             elif t == 1:
@@ -377,59 +411,130 @@
         w_b[at] = cour_v[planes, rows] * value
 
     half = depth // 2
-
-    def grad_copy(to, slot, part_no):
+    side = 4
+    e_y, e_x = e // side, lax.rem(e, side)
+    mine = ((e_y, e_x), (e_x, e_y))
+
+    def owner(way, p, q):
+        return p * side + q if way == 0 else q * side + p
+
+    def first_copy(way, to, slot):
         return pltpu.make_async_remote_copy(
-            src_ref=gsend.at[part_no, to],
-            dst_ref=grecv.at[part_no, slot],
-            send_sem=grad_send.at[part_no, to],
-            recv_sem=grad_recv.at[part_no, slot],
+            src_ref=gsend.at[way, to],
+            dst_ref=gfirst.at[way, slot],
+            send_sem=first_send.at[way, to],
+            recv_sem=first_recv.at[way, slot],
+            device_id={"enc": owner(way, to, mine[way][1])},
+            device_id_type=MESH,
+        )
+
+    def last_copy(way, to, slot):
+        return pltpu.make_async_remote_copy(
+            src_ref=gsum.at[way, to],
+            dst_ref=glast.at[way, slot],
+            send_sem=last_send.at[way, to],
+            recv_sem=last_recv.at[way, slot],
+            device_id={"enc": owner(way, mine[way][0], to)},
+            device_id_type=MESH,
+        )
+
+    def face_copy(to, slot):
+        return pltpu.make_async_remote_copy(
+            src_ref=fsend.at[to],
+            dst_ref=frecv.at[slot],
+            send_sem=face_send.at[to],
+            recv_sem=face_recv.at[slot],
             device_id={"enc": to},
             device_id_type=MESH,
         )
 
-    def last_adjoint(part_no, blocks):
+    def last_adjoint(z0, nz, j):
+        x0 = pl.multiple_of(j * 8, 8)
+        rows = pl.ds(x0, 8)
+        planes = pl.ds(z0, nz)
+        _, along = laplace(w_b, z0, nz, x0, 8)
+        value = a_1[planes, rows]
+        value = (value + value - a_4[planes, rows]) + along + inject[0, planes, rows]
+        adj_first[0, planes, rows] = value
+        return grad[planes, rows] + value * image_0[planes, rows]
+
+    def last_middle():
+        for off in (2, 1, 3, 0):
+            to = lax.rem(e_y + off, side)
+
+            def tile(q, carry):
+                value = last_adjoint(HALO, half, to * side + q)
+                gsend[0, to, q] = value[: half // 2]
+                gsend[1, q, to] = value[half // 2 :]
+                return carry
+
+            lax.fori_loop(0, side, tile, 0, unroll=LAST_UNROLL)
+            if off != 0:
+                first_copy(0, to, e_y).start()
+        for off in (2, 1, 3):
+            first_copy(1, lax.rem(e_x + off, side), e_x).start()
+
+    def last_faces():
         def tile(i, carry):
             j = lax.rem(e + 1 + i, n)
-            x0 = pl.multiple_of(j * 8, 8)
-            rows = pl.ds(x0, 8)
-            put = 0
-            for z0, nz in blocks:
-                planes = pl.ds(z0, nz)
-                _, along = laplace(w_b, z0, nz, x0, 8)
-                value = a_1[planes, rows]
-                value = (value + value - a_4[planes, rows]) + along + inject[0, planes, rows]
-                a_4[planes, rows] = value
-                gsend[part_no, j, pl.ds(put, nz)] = (
-                    grad[planes, rows] + value * image_0[planes, rows]
-                )
-                put += nz
+            fsend[j, pl.ds(0, HALO)] = last_adjoint(0, HALO, j)
+            fsend[j, pl.ds(HALO, HALO)] = last_adjoint(depth - HALO, HALO, j)
 
             @pl.when(j != e)
             def _():
-                grad_copy(j, e, part_no).start()
+                face_copy(j, e).start()
 
             return carry
 
         lax.fori_loop(0, n, tile, 0, unroll=LAST_UNROLL)
 
-    loads[0].wait()
+    def first_sum(way):
+        p, q = mine[way]
+        total = gsend[way, p]
+        for off in range(1, side):
+            slot = lax.rem(p + off, side)
+            first_copy(way, slot, slot).wait_recv()
+            total = total + gfirst[way, slot]
+        gsum[way] = total
+        for off in range(1, side):
+            last_copy(way, lax.rem(q + off, side), q).start()
+
+    scale = 1.0 / (UNIT * steps * n)
+
+    def last_sum(way):
+        q = mine[way][1]
+        total = gsum[way, q]
+        for off in range(1, side):
+            slot = lax.rem(q + off, side)
+            last_copy(way, slot, slot).wait_recv()
+            total = total + glast[way, slot]
+        gradient[pl.ds(HALO + way * (half // 2), half // 2)] = total * scale
+
+    def face_sum():
+        def add(k, total):
+            slot = lax.rem(e + k, n)
+            face_copy(slot, slot).wait_recv()
+            return total + frecv[slot]
+
+        total = lax.fori_loop(1, n, add, fsend[e]) * scale
+        gradient[pl.ds(0, HALO)] = total[:HALO]
+        gradient[pl.ds(depth - HALO, HALO)] = total[HALO:]
+
     loads[4].wait()
     loads[5].wait()
     work = forward(0, u_a, u_b)
     sweep(middle, work)
-    halo_wait(0, fwd_now, u_a)
+    halo_wait(0, u_a)
     sweep(faces, work)
     work = adjoint(3, w_a, w_b, a_4, a_5, a_5)
     sweep(middle, work)
-    halo_wait(1, w_a, w_a)
+    halo_wait(1, w_a)
     sweep(faces, work)
 
     lax.fori_loop(1, n, enc_wait, 0)
-    pattern[...] = jnp.zeros(pattern.shape, F32)
-    lax.fori_loop(0, n // group, sources, 0)
+    sources()
     sweep(faces, add_pattern)
-    halo_start(2, u_b, u_b)
+    halo_start(2, u_b)
     sweep(middle, add_pattern)
 
     total = parts[0]
@@ -438,82 +543,82 @@
     traces_v[...] = total * (1.0 / (shots * n) ** 0.5)
     receivers(3)
     sweep(faces, add_inject)
-    halo_start(3, w_b, w_b)
+    halo_start(3, w_b)
     sweep(middle, add_inject)
     for t in range(3):
         receivers(2 - t)
 
-    halo_sent(0, fwd_now, u_a)
+    halo_sent(0, u_a)
     work = forward(1, u_b, u_a)
-    halo_wait(2, u_b, u_b)
+    halo_wait(2, u_b)
     sweep(faces, work)
-    halo_start(4, u_a, u_a)
+    halo_start(4, u_a)
     sweep(middle, work)
 
-    halo_sent(1, w_a, w_a)
+    halo_sent(1, w_a)
     work = adjoint(2, w_b, w_a, a_5, a_4, a_4)
-    halo_wait(3, w_b, w_b)
+    halo_wait(3, w_b)
     sweep(faces, work)
-    halo_start(5, w_a, w_a)
+    halo_start(5, w_a)
     sweep(middle, work)
 
-    halo_sent(2, u_b, u_b)
+    halo_sent(2, u_b)
     work = forward(2, u_a, u_b)
-    halo_wait(4, u_a, u_a)
+    halo_wait(4, u_a)
     sweep(faces, work)
-    halo_start(6, u_b, u_b)
+    halo_start(6, u_b)
     sweep(middle, work)
 
-    halo_sent(3, w_b, w_b)
+    halo_sent(3, w_b)
     work = adjoint(1, w_a, w_b, a_4, a_5, a_1)
-    halo_wait(5, w_a, w_a)
+    halo_wait(5, w_a)
     sweep(faces, work)
-    halo_start(7, w_b, w_b)
+    halo_start(7, w_b)
     sweep(middle, work)
 
-    halo_sent(4, u_a, u_a)
+    halo_sent(4, u_a)
     work = forward(3, u_b, u_a)
     sweep(middle, work)
-    halo_wait(6, u_b, u_b)
+    halo_wait(6, u_b)
     sweep(faces, work)
-    store_u = pltpu.make_async_copy(u_a.at[inner, body_rows, :], fwd_last.at[0], store_sem.at[0])
-    store_u.start()
-
-    last_adjoint(0, middle)
-    halo_wait(7, w_b, w_b)
-    last_adjoint(1, faces)
-    store_a = pltpu.make_async_copy(a_4, adj_first.at[0], store_sem.at[1])
-    store_a.start()
-
-    def grad_sum(part_no):
-        def grad_wait(k, share):
-            slot = lax.rem(e + k, n)
-            grad_copy(slot, slot, part_no).wait_recv()
-            return share + grecv[part_no, slot]
-
-        return lax.fori_loop(1, n, grad_wait, gsend[part_no, e]) * (1.0 / (UNIT * steps * n))
-
-    gout[pl.ds(HALO, half)] = grad_sum(0)
-    share = grad_sum(1)
-    gout[pl.ds(0, HALO)] = share[:HALO]
-    gout[pl.ds(depth - HALO, HALO)] = share[HALO:]
-    store_g = pltpu.make_async_copy(gout, gradient, store_sem.at[2])
-    store_g.start()
+
+    last_middle()
+    halo_wait(7, w_b)
+    last_faces()
+    first_sum(0)
+    first_sum(1)
+    face_sum()
+    last_sum(0)
+    last_sum(1)
 
     def finish(k, carry):
         enc_copy(k, False).wait_send()
         to = lax.rem(e + k, n)
-        grad_copy(to, to, 0).wait_send()
-        grad_copy(to, to, 1).wait_send()
+        face_copy(to, to).wait_send()
         return carry
 
     lax.fori_loop(1, n, finish, 0)
-    halo_sent(5, w_a, w_a)
-    halo_sent(6, u_b, u_b)
-    halo_sent(7, w_b, w_b)
-    store_u.wait()
-    store_a.wait()
-    store_g.wait()
+    for way in range(2):
+        for off in range(1, side):
+            to = lax.rem(mine[way][0] + off, side)
+            first_copy(way, to, to).wait_send()
+            to = lax.rem(mine[way][1] + off, side)
+            last_copy(way, to, to).wait_send()
+    halo_sent(5, w_a)
+    halo_sent(6, u_b)
+    halo_sent(7, w_b)
+
+
+def store(share, fwd, adj, gradient, fwd_last, adj_first, sem):
+    copies = [
+        pltpu.make_async_copy(share, gradient, sem.at[0]),
+        pltpu.make_async_copy(fwd, fwd_last, sem.at[1]),
+        pltpu.make_async_copy(adj, adj_first, sem.at[2]),
+    ]
+    for copy in copies:
+        copy.start()
+    for copy in copies:
+        copy.wait()
 
 
 def body(
@@ -535,15 +640,15 @@
     share = (depth, width // n, length)
     field = pltpu.VMEM((depth, width, length), F32)
     padded = pltpu.VMEM((depth + 2 * HALO, width + 2 * PAD, length), F32)
-    hot = max(2 * recvs, 4 * shots)
+    hot = max(2 * recvs, n * shots)
     anywhere = pl.BlockSpec(memory_space=pl.ANY)
     vmem = pl.BlockSpec(memory_space=pltpu.VMEM)
-    return pl.pallas_call(
+    results = pl.pallas_call(
         functools.partial(kernel, n, nd),
         out_shape=(
-            jax.ShapeDtypeStruct(share, F32),
-            jax.ShapeDtypeStruct((1, depth, width, length), F32),
-            jax.ShapeDtypeStruct((1, depth, width, length), F32),
+            pltpu.VMEM(share, F32),
+            pltpu.VMEM((1, depth, width, length), F32),
+            pltpu.VMEM((1, depth, width, length), F32),
         ),
         in_specs=[
             anywhere,
@@ -557,7 +662,7 @@
             anywhere,
             anywhere,
         ],
-        out_specs=(anywhere, anywhere, anywhere),
+        out_specs=(vmem, vmem, vmem),
         scratch_shapes=[
             pltpu.VMEM((shots, steps, recvs), BF16),
             field,
@@ -574,26 +679,34 @@
             field,
             pltpu.VMEM((steps, depth, width, length), F32),
             pltpu.VMEM((2 * length, length), BF16),
-            pltpu.VMEM((n // 4, 4 * width, 4 * shots), BF16),
+            pltpu.VMEM((4 * width, n * shots), BF16),
             pltpu.VMEM((4 * width, 2 * recvs), BF16),
             pltpu.VMEM((4 * length, hot), BF16),
             pltpu.VMEM((n, 8, recvs), F32),
             pltpu.VMEM((n, 8, recvs), F32),
             pltpu.VMEM((8, recvs), F32),
-            pltpu.VMEM((2, n, depth // 2) + share[1:], F32),
-            pltpu.VMEM((2, n, depth // 2) + share[1:], F32),
-            pltpu.VMEM(share, F32),
+            pltpu.VMEM((2, 4, 4, depth // 4) + share[1:], F32),
+            pltpu.VMEM((2, 4, 4, depth // 4) + share[1:], F32),
+            pltpu.VMEM((2, 4, depth // 4) + share[1:], F32),
+            pltpu.VMEM((2, 4, depth // 4) + share[1:], F32),
+            pltpu.VMEM((n, depth // 2) + share[1:], F32),
+            pltpu.VMEM((n, depth // 2) + share[1:], F32),
+            pltpu.VMEM((8, 2, HALO - 1, width, length), BF16),
+            pltpu.VMEM((8, 2, HALO - 1, width, length), BF16),
             pltpu.SemaphoreType.DMA((6,)),
-            pltpu.SemaphoreType.DMA((3,)),
             pltpu.SemaphoreType.DMA((n,)),
             pltpu.SemaphoreType.DMA((n,)),
-            pltpu.SemaphoreType.DMA((8, 2)),
-            pltpu.SemaphoreType.DMA((8, 2)),
-            pltpu.SemaphoreType.DMA((2, n)),
-            pltpu.SemaphoreType.DMA((2, n)),
+            pltpu.SemaphoreType.DMA((8, 2, 2)),
+            pltpu.SemaphoreType.DMA((8, 2, 2)),
+            pltpu.SemaphoreType.DMA((2, 4)),
+            pltpu.SemaphoreType.DMA((2, 4)),
+            pltpu.SemaphoreType.DMA((2, 4)),
+            pltpu.SemaphoreType.DMA((2, 4)),
+            pltpu.SemaphoreType.DMA((n,)),
+            pltpu.SemaphoreType.DMA((n,)),
         ],
         compiler_params=pltpu.CompilerParams(
-            collective_id=0, has_side_effects=True, vmem_limit_bytes=56 * 2**20
+            collective_id=0, has_side_effects=True, vmem_limit_bytes=58 * 2**20
         ),
     )(
         residual,
@@ -607,6 +720,14 @@
         adj_next,
         adj_now,
     )
+    return pl.pallas_call(
+        store,
+        out_shape=tuple(jax.ShapeDtypeStruct(r.shape, F32) for r in results),
+        in_specs=[vmem] * 3,
+        out_specs=(anywhere,) * 3,
+        scratch_shapes=[pltpu.SemaphoreType.DMA((3,))],
+        compiler_params=pltpu.CompilerParams(vmem_limit_bytes=4 * 2**20),
+    )(*results)
 
 
 def solution(mesh):

time: 59 us -> 48.4 us (0.82)
  Pallas kernels: 52.6 us -> 47.3 us
  local copies, waits for them, and re-layouts: 4.83 us -> 0 us
    pallas_call x1 -> x2, Pallas kernels: 52.6 us -> 47.3 us  [the longest x1 46 us: body(): pl.pallas_call(functools.partial(kernel, n, nd), out_shape=(pltpu.VMEM(sh...]
    unnamed x5 -> x0, local copies, waits for them, and re-layouts: 4.83 us -> none
where the time goes in v2:
time: 48.4 us; the launch traced here: 48 us
  Pallas kernels  47.3 us (98%)
  between operations  0.64 us (1%)
    pallas_call x1, Pallas kernels, body(): pl.pallas_call(functools.partial(kernel, n, nd), out_shape=(pltpu.VMEM(sh...  46 us
    pallas_call x1, Pallas kernels, body(): pl.pallas_call(store, out_shape=tuple((jax.ShapeDtypeStruct(r.shape, F32)...  1.37 us

profile of v2, /device:TPU:128, one launch (start us, length us, event | category | flops | bytes accessed | tf_op | source)
XLA Modules:
  0.0 48.0 jit_solution(10437567943094557307)
XLA Ops:
  0.6 46.0 %shard_map.121 = (f32[16,8,128]{2,1,0:T(8,128)S(1)}, f32[1,16,128,128]{3,2,1,0:T(8,128)S(1)}, f32[1,16,128,128]{3,2,1,0:T(8,128)S(1)}) custom-call(bf16[256,4,512]{2,1,0:T(4,128)(2,1)} %residual.1, s32[16,256]{1,0:T(8,128)} %weights.1, s32[16,1,256]{2,1,0:T(1,128)} %bitcast.2, s32[1,512]{1,0:T(1,128)} %bitcast.3, f32[4]{0:T(128)} %wavelet.1, ...), custom_call_target="tpu_custom_call" | custom-call | tf_op jit(solution)/shard_map/pallas_call | solution.py:646
  46.6 1.4 %shard_map.122 = (f32[16,8,128]{2,1,0:T(8,128)}, f32[1,16,128,128]{3,2,1,0:T(8,128)}, f32[1,16,128,128]{3,2,1,0:T(8,128)}) custom-call(f32[16,8,128]{2,1,0:T(8,128)S(1)} %get-tuple-element.6.share, f32[1,16,128,128]{3,2,1,0:T(8,128)S(1)} %get-tuple-element.7.fwd, f32[1,16,128,128]{3,2,1,0:T(8,128)S(1)} %get-tuple-element.8.adj), custom_call_target="tpu_custom_call" | custom-call | tf_op jit(solution)/shard_map/pallas_call | solution.py:723

commit v3 on v2

--- a/solution.py
+++ b/solution.py
@@ -1,4 +1,5 @@
 import functools
+import math
 
 import jax
 import jax.numpy as jnp
@@ -16,8 +17,7 @@
 PAD = 8
 HALO = 4
 TILE = 16
-UNROLL = 4
-LAST_UNROLL = 4
+UNROLL = 8
 
 
 def kernel(
@@ -57,25 +57,25 @@
     part,
     parts,
     traces_v,
+    sign_out,
+    sign_in,
     gsend,
     gfirst,
     gsum,
     glast,
-    fsend,
-    frecv,
     staged,
     landed,
     load_sem,
     enc_send,
     enc_recv,
+    sign_send,
+    sign_recv,
     halo_send,
     halo_recv,
     first_send,
     first_recv,
     last_send,
     last_recv,
-    face_send,
-    face_recv,
 ):
     depth, width, length = cour_v.shape
     shots = weights.shape[1]
@@ -89,9 +89,9 @@
 
     loads = [
         pltpu.make_async_copy(fwd_now.at[0], u_a.at[inner, body_rows, :], load_sem.at[0]),
+        pltpu.make_async_copy(residual, res_v, load_sem.at[3]),
         pltpu.make_async_copy(adj_now.at[0], a_4, load_sem.at[1]),
         pltpu.make_async_copy(courant, cour_v, load_sem.at[2]),
-        pltpu.make_async_copy(residual, res_v, load_sem.at[3]),
         pltpu.make_async_copy(fwd_prev.at[0], u_b.at[inner, body_rows, :], load_sem.at[4]),
         pltpu.make_async_copy(adj_next.at[0], a_5, load_sem.at[5]),
     ]
@@ -128,18 +128,6 @@
         @pl.when(d == nd - 1)
         def _():
             field[pl.ds(HALO + depth, HALO)] = jnp.zeros((HALO, width + 2 * PAD, length), F32)
-
-    loads[1].wait()
-    loads[2].wait()
-
-    def scale_tile(j, carry):
-        rows = pl.ds(pl.multiple_of(j * 8, 8), 8)
-        scaled = cour_v[:, rows, :] * (1.0 / UNIT)
-        cour_v[:, rows, :] = scaled
-        w_a[inner, pl.ds(pl.multiple_of(j * 8 + PAD, 8), 8), :] = scaled * a_4[:, rows, :]
-        return carry
-
-    lax.fori_loop(0, width // 8, scale_tile, 0)
 
     def halo_copies(h, field, down):
         way = 0 if down else 1
@@ -207,17 +195,39 @@
                 copy.wait_recv()
             field[pl.ds(0, HALO - 1), body_rows, :] = landed[h, 1].astype(F32)
 
+    signs = weights[...].astype(F32)
+    sign_out[...] = signs.reshape(n, 1, shots)
+    sign_in[e] = sign_out[e]
+
+    def sign_copy(k, incoming):
+        to = lax.rem(e + k, n)
+        slot = lax.rem(e - k + n, n) if incoming else e
+        return pltpu.make_async_remote_copy(
+            src_ref=sign_out.at[to],
+            dst_ref=sign_in.at[slot],
+            send_sem=sign_send.at[k],
+            recv_sem=sign_recv.at[k],
+            device_id={"enc": to},
+            device_id_type=MESH,
+        )
+
+    def sign_start(k, carry):
+        sign_copy(k, False).start()
+        return carry
+
+    def sign_wait(k, carry):
+        sign_copy(k, True).wait_recv()
+        return carry
+
     loads[0].wait()
     halo_stage(0, u_a)
-    halo_stage(1, w_a)
     pl.semaphore_wait(
         barrier, n - 1 + (d > 0).astype(jnp.int32) + (d < nd - 1).astype(jnp.int32)
     )
 
     halo_start(0, u_a, False)
-    halo_start(1, w_a, False)
-
-    signs = weights[...].astype(F32)
+    lax.fori_loop(1, n, sign_start, 0)
+
     shot_of = lax.shift_right_logical(lax.broadcasted_iota(jnp.int32, (shots, shots * steps), 1), 2)
     spread = jnp.where(
         shot_of == lax.broadcasted_iota(jnp.int32, (shots, shots * steps), 0), 1.0, 0.0
@@ -228,20 +238,19 @@
         lax.broadcasted_iota(jnp.int32, (n, 8, shots * steps), 2) & (steps - 1)
     ) == lax.broadcasted_iota(jnp.int32, (n, 8, shots * steps), 1)
     wide = jnp.where(same_step, wide, 0.0).reshape(n * 8, shots * steps).astype(BF16)
-    loads[3].wait()
+    loads[1].wait()
     traces = jnp.dot(
         wide, res_v[...].reshape(shots * steps, recvs), preferred_element_type=F32
     )
     part[...] = traces.reshape(n, 8, recvs)
-    part[:, steps, pl.ds(0, shots)] = signs
     parts[e] = part[e]
 
     def enc_copy(k, incoming):
         to = lax.rem(e + k, n)
         slot = lax.rem(e - k + n, n) if incoming else e
         return pltpu.make_async_remote_copy(
-            src_ref=part.at[to],
-            dst_ref=parts.at[slot],
+            src_ref=part.at[to, pl.ds(0, steps)],
+            dst_ref=parts.at[slot, pl.ds(0, steps)],
             send_sem=enc_send.at[k],
             recv_sem=enc_recv.at[k],
             device_id={"enc": to},
@@ -253,6 +262,19 @@
         return carry
 
     lax.fori_loop(1, n, enc_start, 0)
+
+    loads[2].wait()
+    loads[3].wait()
+
+    def scale_tile(j, carry):
+        rows = pl.ds(pl.multiple_of(j * 8, 8), 8)
+        scaled = cour_v[:, rows, :] * (1.0 / UNIT)
+        cour_v[:, rows, :] = scaled
+        w_a[inner, pl.ds(pl.multiple_of(j * 8 + PAD, 8), 8), :] = scaled * a_4[:, rows, :]
+        return carry
+
+    lax.fori_loop(0, width // 8, scale_tile, 0)
+    halo_start(1, w_a)
 
     across = lax.broadcasted_iota(jnp.int32, (2 * length, length), 0) & (length - 1)
     gap = jnp.abs(across - lax.broadcasted_iota(jnp.int32, (2 * length, length), 1))
@@ -299,7 +321,7 @@
 
     def source_cols(i, carry):
         cell = source_pos[i] - base
-        sign = parts[i, steps : steps + 1, pl.ds(0, shots)]
+        sign = sign_in[i]
         cols_hot[:, pl.ds(pl.multiple_of(i * shots, shots), shots)] = jnp.where(
             lax.broadcasted_iota(jnp.int32, (hot_cols, shots), 0) == col_of(cell), sign, 0.0
         ).astype(BF16)
@@ -357,14 +379,14 @@
 
         lax.fori_loop(0, width // TILE, tile, 0, unroll=unroll)
 
-    def forward(t, now, prev):
+    def forward(t, now, prev, bare=False):
         def work(z0, nz, x0):
             planes = pl.ds(z0, nz)
             rows = pl.ds(x0, TILE)
             at = (pl.ds(z0 + HALO, nz), pl.ds(pl.multiple_of(x0 + PAD, 8), TILE))
             mid, image = laplace(now, z0, nz, x0, TILE)
             value = (mid + mid - prev[at]) + cour_v[planes, rows] * image
-            if t > 0:
+            if not bare:
                 value = value + wavelet[t] * pattern[planes, rows]
             if t < steps - 1:
                 prev[at] = value
@@ -385,14 +407,14 @@
         at = (pl.ds(z0 + HALO, nz), pl.ds(pl.multiple_of(x0 + PAD, 8), TILE))
         u_b[at] += wavelet[0] * pattern[pl.ds(z0, nz), pl.ds(x0, TILE)]
 
-    def adjoint(t, w_now, w_next, now, later, new):
+    def adjoint(t, w_now, w_next, now, later, new, bare=False):
         def work(z0, nz, x0):
             planes = pl.ds(z0, nz)
             rows = pl.ds(x0, TILE)
             _, along = laplace(w_now, z0, nz, x0, TILE)
             value = now[planes, rows]
             value = (value + value - later[planes, rows]) + along
-            if t < steps - 1:
+            if not bare:
                 value = value + inject[t, planes, rows]
                 at = (pl.ds(z0 + HALO, nz), pl.ds(pl.multiple_of(x0 + PAD, 8), TILE))
                 w_next[at] = cour_v[planes, rows] * value
@@ -411,139 +433,106 @@
         w_b[at] = cour_v[planes, rows] * value
 
     half = depth // 2
-    side = 4
+    side = math.isqrt(n)
     e_y, e_x = e // side, lax.rem(e, side)
     mine = ((e_y, e_x), (e_x, e_y))
 
     def owner(way, p, q):
         return p * side + q if way == 0 else q * side + p
 
-    def first_copy(way, to, slot):
+    def first_copy(group, way, to, slot):
         return pltpu.make_async_remote_copy(
-            src_ref=gsend.at[way, to],
-            dst_ref=gfirst.at[way, slot],
-            send_sem=first_send.at[way, to],
-            recv_sem=first_recv.at[way, slot],
+            src_ref=gsend.at[group, way, to],
+            dst_ref=gfirst.at[group, way, slot],
+            send_sem=first_send.at[group, way, to],
+            recv_sem=first_recv.at[group, way, slot],
             device_id={"enc": owner(way, to, mine[way][1])},
             device_id_type=MESH,
         )
 
-    def last_copy(way, to, slot):
+    def last_copy(group, way, to, slot):
         return pltpu.make_async_remote_copy(
-            src_ref=gsum.at[way, to],
-            dst_ref=glast.at[way, slot],
-            send_sem=last_send.at[way, to],
-            recv_sem=last_recv.at[way, slot],
+            src_ref=gsum.at[group, way, to],
+            dst_ref=glast.at[group, way, slot],
+            send_sem=last_send.at[group, way, to],
+            recv_sem=last_recv.at[group, way, slot],
             device_id={"enc": owner(way, mine[way][0], to)},
             device_id_type=MESH,
         )
 
-    def face_copy(to, slot):
-        return pltpu.make_async_remote_copy(
-            src_ref=fsend.at[to],
-            dst_ref=frecv.at[slot],
-            send_sem=face_send.at[to],
-            recv_sem=face_recv.at[slot],
-            device_id={"enc": to},
-            device_id_type=MESH,
-        )
-
-    def last_adjoint(z0, nz, j):
-        x0 = pl.multiple_of(j * 8, 8)
-        rows = pl.ds(x0, 8)
+    span = side * 8
+
+    def last_adjoint(z0, nz, x0, nx):
+        rows = pl.ds(x0, nx)
         planes = pl.ds(z0, nz)
-        _, along = laplace(w_b, z0, nz, x0, 8)
+        _, along = laplace(w_b, z0, nz, x0, nx)
         value = a_1[planes, rows]
         value = (value + value - a_4[planes, rows]) + along + inject[0, planes, rows]
         adj_first[0, planes, rows] = value
         return grad[planes, rows] + value * image_0[planes, rows]
 
-    def last_middle():
-        for off in (2, 1, 3, 0):
+    others = (2, 1, 3) if side == 4 else tuple(range(1, side))
+
+    def last_step(group):
+        for off in others + (0,):
             to = lax.rem(e_y + off, side)
 
-            def tile(q, carry):
-                value = last_adjoint(HALO, half, to * side + q)
-                gsend[0, to, q] = value[: half // 2]
-                gsend[1, q, to] = value[half // 2 :]
-                return carry
-
-            lax.fori_loop(0, side, tile, 0, unroll=LAST_UNROLL)
+            for at in range(0, span, TILE):
+                x0 = pl.multiple_of(to * span + at, 8)
+                if group == 0:
+                    value = last_adjoint(HALO, half, x0, TILE)
+                    lower, upper = value[:HALO], value[HALO:]
+                else:
+                    lower = last_adjoint(0, HALO, x0, TILE)
+                    upper = last_adjoint(depth - HALO, HALO, x0, TILE)
+                for r in range(TILE // 8):
+                    gsend[group, 0, to, at // 8 + r] = lower[:, r * 8 : r * 8 + 8]
+                    gsend[group, 1, at // 8 + r, to] = upper[:, r * 8 : r * 8 + 8]
             if off != 0:
-                first_copy(0, to, e_y).start()
-        for off in (2, 1, 3):
-            first_copy(1, lax.rem(e_x + off, side), e_x).start()
-
-    def last_faces():
-        def tile(i, carry):
-            j = lax.rem(e + 1 + i, n)
-            fsend[j, pl.ds(0, HALO)] = last_adjoint(0, HALO, j)
-            fsend[j, pl.ds(HALO, HALO)] = last_adjoint(depth - HALO, HALO, j)
-
-            @pl.when(j != e)
-            def _():
-                face_copy(j, e).start()
-
-            return carry
-
-        lax.fori_loop(0, n, tile, 0, unroll=LAST_UNROLL)
-
-    def first_sum(way):
+                first_copy(group, 0, to, e_y).start()
+        for off in others:
+            first_copy(group, 1, lax.rem(e_x + off, side), e_x).start()
+
+    def first_sum(group, way):
         p, q = mine[way]
-        total = gsend[way, p]
+        total = gsend[group, way, p]
         for off in range(1, side):
             slot = lax.rem(p + off, side)
-            first_copy(way, slot, slot).wait_recv()
-            total = total + gfirst[way, slot]
-        gsum[way] = total
-        for off in range(1, side):
-            last_copy(way, lax.rem(q + off, side), q).start()
-
-    scale = 1.0 / (UNIT * steps * n)
-
-    def last_sum(way):
+            first_copy(group, way, slot, slot).wait_recv()
+            total = total + gfirst[group, way, slot]
+        gsum[group, way] = total
+        for off in others:
+            last_copy(group, way, lax.rem(q + off, side), q).start()
+
+    def last_sum(group, way):
         q = mine[way][1]
-        total = gsum[way, q]
+        total = gsum[group, way, q]
         for off in range(1, side):
             slot = lax.rem(q + off, side)
-            last_copy(way, slot, slot).wait_recv()
-            total = total + glast[way, slot]
-        gradient[pl.ds(HALO + way * (half // 2), half // 2)] = total * scale
-
-    def face_sum():
-        def add(k, total):
-            slot = lax.rem(e + k, n)
-            face_copy(slot, slot).wait_recv()
-            return total + frecv[slot]
-
-        total = lax.fori_loop(1, n, add, fsend[e]) * scale
-        gradient[pl.ds(0, HALO)] = total[:HALO]
-        gradient[pl.ds(depth - HALO, HALO)] = total[HALO:]
+            last_copy(group, way, slot, slot).wait_recv()
+            total = total + glast[group, way, slot]
+        z0 = HALO * (1 + way) if group == 0 else way * (depth - HALO)
+        gradient[pl.ds(z0, HALO)] = total * (1.0 / (UNIT * steps * n))
 
     loads[4].wait()
     loads[5].wait()
-    work = forward(0, u_a, u_b)
-    sweep(middle, work)
+    sweep(middle, forward(0, u_a, u_b, True))
+    sweep(middle, adjoint(3, w_a, None, a_4, a_5, a_5, True))
+    lax.fori_loop(1, n, sign_wait, 0)
+    sources()
     halo_wait(0, u_a)
-    sweep(faces, work)
-    work = adjoint(3, w_a, w_b, a_4, a_5, a_5)
-    sweep(middle, work)
-    halo_wait(1, w_a)
-    sweep(faces, work)
-
+    sweep(faces, forward(0, u_a, u_b))
+    halo_start(2, u_b)
     lax.fori_loop(1, n, enc_wait, 0)
-    sources()
-    sweep(faces, add_pattern)
-    halo_start(2, u_b)
-    sweep(middle, add_pattern)
-
-    total = parts[0]
+    total = parts[0, pl.ds(0, steps)]
     for i in range(1, n):
-        total = total + parts[i]
+        total = total + parts[i, pl.ds(0, steps)]
     traces_v[...] = total * (1.0 / (shots * n) ** 0.5)
     receivers(3)
-    sweep(faces, add_inject)
+    halo_wait(1, w_a)
+    sweep(faces, adjoint(3, w_a, w_b, a_4, a_5, a_5))
     halo_start(3, w_b)
+    sweep(middle, add_pattern)
     sweep(middle, add_inject)
     for t in range(3):
         receivers(2 - t)
@@ -582,28 +571,29 @@
     halo_wait(6, u_b)
     sweep(faces, work)
 
-    last_middle()
+    last_step(0)
     halo_wait(7, w_b)
-    last_faces()
-    first_sum(0)
-    first_sum(1)
-    face_sum()
-    last_sum(0)
-    last_sum(1)
+    last_step(1)
+    for group in range(2):
+        for way in range(2):
+            first_sum(group, way)
+    for group in range(2):
+        for way in range(2):
+            last_sum(group, way)
 
     def finish(k, carry):
         enc_copy(k, False).wait_send()
-        to = lax.rem(e + k, n)
-        face_copy(to, to).wait_send()
+        sign_copy(k, False).wait_send()
         return carry
 
     lax.fori_loop(1, n, finish, 0)
-    for way in range(2):
-        for off in range(1, side):
-            to = lax.rem(mine[way][0] + off, side)
-            first_copy(way, to, to).wait_send()
-            to = lax.rem(mine[way][1] + off, side)
-            last_copy(way, to, to).wait_send()
+    for group in range(2):
+        for way in range(2):
+            for off in others:
+                to = lax.rem(mine[way][0] + off, side)
+                first_copy(group, way, to, to).wait_send()
+                to = lax.rem(mine[way][1] + off, side)
+                last_copy(group, way, to, to).wait_send()
     halo_sent(5, w_a)
     halo_sent(6, u_b)
     halo_sent(7, w_b)
@@ -638,6 +628,7 @@
     shots, steps, recvs = residual.shape
     depth, width, length = courant.shape
     share = (depth, width // n, length)
+    side = math.isqrt(n)
     field = pltpu.VMEM((depth, width, length), F32)
     padded = pltpu.VMEM((depth + 2 * HALO, width + 2 * PAD, length), F32)
     hot = max(2 * recvs, n * shots)
@@ -684,26 +675,26 @@
             pltpu.VMEM((4 * length, hot), BF16),
             pltpu.VMEM((n, 8, recvs), F32),
             pltpu.VMEM((n, 8, recvs), F32),
-            pltpu.VMEM((8, recvs), F32),
-            pltpu.VMEM((2, 4, 4, depth // 4) + share[1:], F32),
-            pltpu.VMEM((2, 4, 4, depth // 4) + share[1:], F32),
-            pltpu.VMEM((2, 4, depth // 4) + share[1:], F32),
-            pltpu.VMEM((2, 4, depth // 4) + share[1:], F32),
-            pltpu.VMEM((n, depth // 2) + share[1:], F32),
-            pltpu.VMEM((n, depth // 2) + share[1:], F32),
+            pltpu.VMEM((steps, recvs), F32),
+            pltpu.VMEM((n, 1, shots), F32),
+            pltpu.VMEM((n, 1, shots), F32),
+            pltpu.VMEM((2, 2, side, side, HALO) + share[1:], F32),
+            pltpu.VMEM((2, 2, side, side, HALO) + share[1:], F32),
+            pltpu.VMEM((2, 2, side, HALO) + share[1:], F32),
+            pltpu.VMEM((2, 2, side, HALO) + share[1:], F32),
             pltpu.VMEM((8, 2, HALO - 1, width, length), BF16),
             pltpu.VMEM((8, 2, HALO - 1, width, length), BF16),
             pltpu.SemaphoreType.DMA((6,)),
             pltpu.SemaphoreType.DMA((n,)),
             pltpu.SemaphoreType.DMA((n,)),
+            pltpu.SemaphoreType.DMA((n,)),
+            pltpu.SemaphoreType.DMA((n,)),
             pltpu.SemaphoreType.DMA((8, 2, 2)),
             pltpu.SemaphoreType.DMA((8, 2, 2)),
-            pltpu.SemaphoreType.DMA((2, 4)),
-            pltpu.SemaphoreType.DMA((2, 4)),
-            pltpu.SemaphoreType.DMA((2, 4)),
-            pltpu.SemaphoreType.DMA((2, 4)),
-            pltpu.SemaphoreType.DMA((n,)),
-            pltpu.SemaphoreType.DMA((n,)),
+            pltpu.SemaphoreType.DMA((2, 2, side)),
+            pltpu.SemaphoreType.DMA((2, 2, side)),
+            pltpu.SemaphoreType.DMA((2, 2, side)),
+            pltpu.SemaphoreType.DMA((2, 2, side)),
         ],
         compiler_params=pltpu.CompilerParams(
             collective_id=0, has_side_effects=True, vmem_limit_bytes=58 * 2**20

time: 48.4 us -> 47.3 us (0.977)
  Pallas kernels: 47.3 us -> 46.3 us
    pallas_call x1, Pallas kernels: 46 us -> 45 us  [body(): pl.pallas_call(functools.partial(kernel, n, nd), out_shape=(pltpu.VMEM(sh...]
where the time goes in v3:
time: 47.3 us; the launch traced here: 47.1 us
  Pallas kernels  46.3 us (98%)
  between operations  0.8 us (2%)
    pallas_call x1, Pallas kernels, body(): pl.pallas_call(functools.partial(kernel, n, nd), out_shape=(pltpu.VMEM(sh...  45 us
    pallas_call x1, Pallas kernels, body(): pl.pallas_call(store, out_shape=tuple((jax.ShapeDtypeStruct(r.shape, F32)...  1.37 us

profile of v3, /device:TPU:128, one launch (start us, length us, event | category | flops | bytes accessed | tf_op | source)
XLA Modules:
  0.0 47.1 jit_solution(6968220957560268531)
XLA Ops:
  0.6 45.0 %shard_map.121 = (f32[16,8,128]{2,1,0:T(8,128)S(1)}, f32[1,16,128,128]{3,2,1,0:T(8,128)S(1)}, f32[1,16,128,128]{3,2,1,0:T(8,128)S(1)}) custom-call(bf16[256,4,512]{2,1,0:T(4,128)(2,1)} %residual.1, s32[16,256]{1,0:T(8,128)} %weights.1, s32[16,1,256]{2,1,0:T(1,128)} %bitcast.2, s32[1,512]{1,0:T(1,128)} %bitcast.3, f32[4]{0:T(128)} %wavelet.1, ...), custom_call_target="tpu_custom_call" | custom-call | tf_op jit(solution)/shard_map/pallas_call | solution.py:637
  45.6 1.4 %shard_map.122 = (f32[16,8,128]{2,1,0:T(8,128)}, f32[1,16,128,128]{3,2,1,0:T(8,128)}, f32[1,16,128,128]{3,2,1,0:T(8,128)}) custom-call(f32[16,8,128]{2,1,0:T(8,128)S(1)} %get-tuple-element.6.share, f32[1,16,128,128]{3,2,1,0:T(8,128)S(1)} %get-tuple-element.7.fwd, f32[1,16,128,128]{3,2,1,0:T(8,128)S(1)} %get-tuple-element.8.adj), custom_call_target="tpu_custom_call" | custom-call | tf_op jit(solution)/shard_map/pallas_call | solution.py:714

commit v4 on v3

--- a/solution.py
+++ b/solution.py
@@ -129,71 +129,77 @@
         def _():
             field[pl.ds(HALO + depth, HALO)] = jnp.zeros((HALO, width + 2 * PAD, length), F32)
 
-    def halo_copies(h, field, down):
+    rows_half = width // 2
+
+    def halo_copies(h, field, down, part_no):
         way = 0 if down else 1
         to = {"dom": d - 1 if down else d + 1}
-        face = field.at[HALO if down else HALO + depth - 1, body_rows, :]
-        land = field.at[HALO + depth if down else HALO - 1, body_rows, :]
+        rows = pl.ds(PAD + part_no * rows_half, rows_half)
+        face = field.at[HALO if down else HALO + depth - 1, rows, :]
+        land = field.at[HALO + depth if down else HALO - 1, rows, :]
         return (
             pltpu.make_async_remote_copy(
                 src_ref=face,
                 dst_ref=land,
-                send_sem=halo_send.at[h, way, 0],
-                recv_sem=halo_recv.at[h, way, 0],
+                send_sem=halo_send.at[h, way, part_no, 0],
+                recv_sem=halo_recv.at[h, way, part_no, 0],
                 device_id=to,
                 device_id_type=MESH,
             ),
             pltpu.make_async_remote_copy(
-                src_ref=staged.at[h, way],
-                dst_ref=landed.at[h, way],
-                send_sem=halo_send.at[h, way, 1],
-                recv_sem=halo_recv.at[h, way, 1],
+                src_ref=staged.at[h, way, part_no],
+                dst_ref=landed.at[h, way, part_no],
+                send_sem=halo_send.at[h, way, part_no, 1],
+                recv_sem=halo_recv.at[h, way, part_no, 1],
                 device_id=to,
                 device_id_type=MESH,
             ),
         )
 
-    def halo_stage(h, field):
-        staged[h, 0] = field[pl.ds(HALO + 1, HALO - 1), body_rows, :].astype(BF16)
-        staged[h, 1] = field[pl.ds(depth, HALO - 1), body_rows, :].astype(BF16)
-
-    def halo_start(h, field, stage=True):
-        if stage:
-            halo_stage(h, field)
-
+    def halo_stage(h, field, part_no):
+        rows = pl.ds(PAD + part_no * rows_half, rows_half)
+        staged[h, 0, part_no] = field[pl.ds(HALO + 1, HALO - 1), rows, :].astype(BF16)
+        staged[h, 1, part_no] = field[pl.ds(depth, HALO - 1), rows, :].astype(BF16)
+
+    def halo_start(h, field, part_no):
         @pl.when(d > 0)
         def _():
-            for copy in halo_copies(h, field, True):
+            for copy in halo_copies(h, field, True, part_no):
                 copy.start()
 
         @pl.when(d < nd - 1)
         def _():
-            for copy in halo_copies(h, field, False):
+            for copy in halo_copies(h, field, False, part_no):
                 copy.start()
 
     def halo_sent(h, field):
-        @pl.when(d > 0)
-        def _():
-            for copy in halo_copies(h, field, True):
-                copy.wait_send()
-
-        @pl.when(d < nd - 1)
-        def _():
-            for copy in halo_copies(h, field, False):
-                copy.wait_send()
+        for part_no in range(2):
+
+            @pl.when(d > 0)
+            def _():
+                for copy in halo_copies(h, field, True, part_no):
+                    copy.wait_send()
+
+            @pl.when(d < nd - 1)
+            def _():
+                for copy in halo_copies(h, field, False, part_no):
+                    copy.wait_send()
 
     def halo_wait(h, field):
-        @pl.when(d < nd - 1)
-        def _():
-            for copy in halo_copies(h, field, True):
-                copy.wait_recv()
-            field[pl.ds(HALO + depth + 1, HALO - 1), body_rows, :] = landed[h, 0].astype(F32)
-
-        @pl.when(d > 0)
-        def _():
-            for copy in halo_copies(h, field, False):
-                copy.wait_recv()
-            field[pl.ds(0, HALO - 1), body_rows, :] = landed[h, 1].astype(F32)
+        for part_no in range(2):
+            rows = pl.ds(PAD + part_no * rows_half, rows_half)
+
+            @pl.when(d < nd - 1)
+            def _():
+                for copy in halo_copies(h, field, True, part_no):
+                    copy.wait_recv()
+                field[pl.ds(HALO + depth + 1, HALO - 1), rows, :] = landed[h, 0, part_no].astype(F32)
+
+            @pl.when(d > 0)
+            def _():
+                for copy in halo_copies(h, field, False, part_no):
+                    copy.wait_recv()
+                field[pl.ds(0, HALO - 1), rows, :] = landed[h, 1, part_no].astype(F32)
 
     signs = weights[...].astype(F32)
     sign_out[...] = signs.reshape(n, 1, shots)
@@ -220,12 +226,14 @@
         return carry
 
     loads[0].wait()
-    halo_stage(0, u_a)
+    halo_stage(0, u_a, 0)
+    halo_stage(0, u_a, 1)
     pl.semaphore_wait(
         barrier, n - 1 + (d > 0).astype(jnp.int32) + (d < nd - 1).astype(jnp.int32)
     )
 
-    halo_start(0, u_a, False)
+    halo_start(0, u_a, 0)
+    halo_start(0, u_a, 1)
     lax.fori_loop(1, n, sign_start, 0)
 
     shot_of = lax.shift_right_logical(lax.broadcasted_iota(jnp.int32, (shots, shots * steps), 1), 2)
@@ -274,7 +282,9 @@
         return carry
 
     lax.fori_loop(0, width // 8, scale_tile, 0)
-    halo_start(1, w_a)
+    for part_no in range(2):
+        halo_stage(1, w_a, part_no)
+        halo_start(1, w_a, part_no)
 
     across = lax.broadcasted_iota(jnp.int32, (2 * length, length), 0) & (length - 1)
     gap = jnp.abs(across - lax.broadcasted_iota(jnp.int32, (2 * length, length), 1))
@@ -378,6 +388,19 @@
             return carry
 
         lax.fori_loop(0, width // TILE, tile, 0, unroll=unroll)
+
+    def face_sweep(work, h, field):
+        for part_no in range(2):
+
+            def tile(j, carry):
+                x0 = pl.multiple_of(j * TILE + part_no * rows_half, TILE)
+                for z0, nz in faces:
+                    work(z0, nz, x0)
+                return carry
+
+            lax.fori_loop(0, rows_half // TILE, tile, 0, unroll=4)
+            halo_stage(h, field, part_no)
+            halo_start(h, field, part_no)
 
     def forward(t, now, prev, bare=False):
         def work(z0, nz, x0):
@@ -521,8 +544,7 @@
     lax.fori_loop(1, n, sign_wait, 0)
     sources()
     halo_wait(0, u_a)
-    sweep(faces, forward(0, u_a, u_b))
-    halo_start(2, u_b)
+    face_sweep(forward(0, u_a, u_b), 2, u_b)
     lax.fori_loop(1, n, enc_wait, 0)
     total = parts[0, pl.ds(0, steps)]
     for i in range(1, n):
@@ -530,8 +552,7 @@
     traces_v[...] = total * (1.0 / (shots * n) ** 0.5)
     receivers(3)
     halo_wait(1, w_a)
-    sweep(faces, adjoint(3, w_a, w_b, a_4, a_5, a_5))
-    halo_start(3, w_b)
+    face_sweep(adjoint(3, w_a, w_b, a_4, a_5, a_5), 3, w_b)
     sweep(middle, add_pattern)
     sweep(middle, add_inject)
     for t in range(3):
@@ -540,38 +561,34 @@
     halo_sent(0, u_a)
     work = forward(1, u_b, u_a)
     halo_wait(2, u_b)
-    sweep(faces, work)
-    halo_start(4, u_a)
+    face_sweep(work, 4, u_a)
     sweep(middle, work)
 
     halo_sent(1, w_a)
     work = adjoint(2, w_b, w_a, a_5, a_4, a_4)
     halo_wait(3, w_b)
-    sweep(faces, work)
-    halo_start(5, w_a)
+    face_sweep(work, 5, w_a)
     sweep(middle, work)
 
     halo_sent(2, u_b)
     work = forward(2, u_a, u_b)
     halo_wait(4, u_a)
-    sweep(faces, work)
-    halo_start(6, u_b)
+    face_sweep(work, 6, u_b)
     sweep(middle, work)
 
     halo_sent(3, w_b)
     work = adjoint(1, w_a, w_b, a_4, a_5, a_1)
     halo_wait(5, w_a)
-    sweep(faces, work)
-    halo_start(7, w_b)
+    face_sweep(work, 7, w_b)
     sweep(middle, work)
 
     halo_sent(4, u_a)
     work = forward(3, u_b, u_a)
     sweep(middle, work)
+    last_step(0)
     halo_wait(6, u_b)
     sweep(faces, work)
 
-    last_step(0)
     halo_wait(7, w_b)
     last_step(1)
     for group in range(2):
@@ -682,15 +699,15 @@
             pltpu.VMEM((2, 2, side, side, HALO) + share[1:], F32),
             pltpu.VMEM((2, 2, side, HALO) + share[1:], F32),
             pltpu.VMEM((2, 2, side, HALO) + share[1:], F32),
-            pltpu.VMEM((8, 2, HALO - 1, width, length), BF16),
-            pltpu.VMEM((8, 2, HALO - 1, width, length), BF16),
+            pltpu.VMEM((8, 2, 2, HALO - 1, width // 2, length), BF16),
+            pltpu.VMEM((8, 2, 2, HALO - 1, width // 2, length), BF16),
             pltpu.SemaphoreType.DMA((6,)),
             pltpu.SemaphoreType.DMA((n,)),
             pltpu.SemaphoreType.DMA((n,)),
             pltpu.SemaphoreType.DMA((n,)),
             pltpu.SemaphoreType.DMA((n,)),
-            pltpu.SemaphoreType.DMA((8, 2, 2)),
-            pltpu.SemaphoreType.DMA((8, 2, 2)),
+            pltpu.SemaphoreType.DMA((8, 2, 2, 2)),
+            pltpu.SemaphoreType.DMA((8, 2, 2, 2)),
             pltpu.SemaphoreType.DMA((2, 2, side)),
             pltpu.SemaphoreType.DMA((2, 2, side)),
             pltpu.SemaphoreType.DMA((2, 2, side)),

time: 47.3 us -> 46.4 us (0.981)
  Pallas kernels: 46.3 us -> 45.5 us
    pallas_call x1, Pallas kernels: 45 us -> 44.1 us  [body(): pl.pallas_call(functools.partial(kernel, n, nd), out_shape=(pltpu.VMEM(sh...]
where the time goes in v4:
time: 46.4 us; the launch traced here: 46.3 us
  Pallas kernels  45.5 us (98%)
  between operations  0.8 us (2%)
    pallas_call x1, Pallas kernels, body(): pl.pallas_call(functools.partial(kernel, n, nd), out_shape=(pltpu.VMEM(sh...  44.1 us
    pallas_call x1, Pallas kernels, body(): pl.pallas_call(store, out_shape=tuple((jax.ShapeDtypeStruct(r.shape, F32)...  1.37 us

profile of v4, /device:TPU:128, one launch (start us, length us, event | category | flops | bytes accessed | tf_op | source)
XLA Modules:
  0.0 46.3 jit_solution(4528502732895511374)
XLA Ops:
  0.6 44.1 %shard_map.121 = (f32[16,8,128]{2,1,0:T(8,128)S(1)}, f32[1,16,128,128]{3,2,1,0:T(8,128)S(1)}, f32[1,16,128,128]{3,2,1,0:T(8,128)S(1)}) custom-call(bf16[256,4,512]{2,1,0:T(4,128)(2,1)} %residual.1, s32[16,256]{1,0:T(8,128)} %weights.1, s32[16,1,256]{2,1,0:T(1,128)} %bitcast.2, s32[1,512]{1,0:T(1,128)} %bitcast.3, f32[4]{0:T(128)} %wavelet.1, ...), custom_call_target="tpu_custom_call" | custom-call | tf_op jit(solution)/shard_map/pallas_call | solution.py:654
  44.7 1.4 %shard_map.122 = (f32[16,8,128]{2,1,0:T(8,128)}, f32[1,16,128,128]{3,2,1,0:T(8,128)}, f32[1,16,128,128]{3,2,1,0:T(8,128)}) custom-call(f32[16,8,128]{2,1,0:T(8,128)S(1)} %get-tuple-element.6.share, f32[1,16,128,128]{3,2,1,0:T(8,128)S(1)} %get-tuple-element.7.fwd, f32[1,16,128,128]{3,2,1,0:T(8,128)S(1)} %get-tuple-element.8.adj), custom_call_target="tpu_custom_call" | custom-call | tf_op jit(solution)/shard_map/pallas_call | solution.py:731
